TPU v7x, 256 devices: a whole 4x4x8 slice. The times are simulated.
256 devices in a mesh: seq: 8 (over z), chan: 8 (over x, core), dp: 4 (over y).
Axes of the slice: x: 4, y: 4, z: 8, core: 2. Of those that a mesh axis runs over, the one named last changes fastest.
Arguments:
- grad_out: bfloat16 [4, 64, 131072], P('dp', 'chan', 'seq'), may hold values from -6 to 6
- input_spectrum: float32 [4, 2, 64, 512, 512], P('dp', None, 'chan', 'seq'), may hold values from -6 to 6
- filter_spectrum: float32 [2, 64, 512, 512], P(None, 'chan', 'seq'), may hold values from -6 to 6
Outputs:
- input_grad: bfloat16 [4, 64, 131072], P('dp', 'chan', 'seq')
- filter_grad: float32 [64, 131072], P('chan', ('seq', 'dp'))
All inputs are finite; a program needn't handle non-finite values.
Results may differ from a plain program's by a relative error of at most 0.001.
Values may be sent and summed in bfloat16 or wider, within the bound.
A program may use at most 128 MiB of HBM per device.

v0:
```python
import math

import jax
import jax.numpy as jnp
from jax import lax
from jax.sharding import PartitionSpec as P

HIGHEST_PRECISION = lax.Precision.HIGHEST


def counting(length):
    return jnp.arange(length, dtype=jnp.int32)


def phase_table(leading, trailing, modulus):
    product = leading[:, None] * trailing[None, :] % modulus
    phase = product.astype(jnp.float32) * (2.0 * math.pi / modulus)
    return (jnp.cos(phase), jnp.sin(phase))


def contract(pattern, left_side, right_side):
    return jnp.einsum(pattern, left_side, right_side, precision=HIGHEST_PRECISION)


def column_forward(signal, column_start, modulus):
    half_rows = signal.shape[1]
    bin_rows = 2 * half_rows
    cosines, sine_values = phase_table(counting(half_rows), counting(bin_rows), bin_rows)
    real_part = contract("cjr,jk->ckr", signal, cosines)
    imaginary = -contract("cjr,jk->ckr", signal, sine_values)
    twist_cosine, twist_sine = phase_table(
        counting(bin_rows), column_start + counting(signal.shape[2]), modulus
    )
    return jnp.stack(
        [
            real_part * twist_cosine + imaginary * twist_sine,
            imaginary * twist_cosine - real_part * twist_sine,
        ]
    )


def row_forward(blocks):
    bin_columns = blocks.shape[-1]
    cosines, sine_values = phase_table(counting(bin_columns), counting(bin_columns), bin_columns)
    real_part = contract("ckr,rq->ckq", blocks[0], cosines) + contract(
        "ckr,rq->ckq", blocks[1], sine_values
    )
    imaginary = contract("ckr,rq->ckq", blocks[1], cosines) - contract(
        "ckr,rq->ckq", blocks[0], sine_values
    )
    return jnp.stack([real_part, imaginary])


def row_inverse(blocks, row_start, modulus):
    bin_columns = blocks.shape[-1]
    cosines, sine_values = phase_table(counting(bin_columns), counting(bin_columns), bin_columns)
    turned_real = contract("ckr,rq->ckq", blocks[0], cosines) - contract(
        "ckr,rq->ckq", blocks[1], sine_values
    )
    turned_imaginary = contract("ckr,rq->ckq", blocks[1], cosines) + contract(
        "ckr,rq->ckq", blocks[0], sine_values
    )
    twist_cosine, twist_sine = phase_table(
        row_start + counting(blocks.shape[2]), counting(bin_columns), modulus
    )
    return jnp.stack(
        [
            turned_real * twist_cosine - turned_imaginary * twist_sine,
            turned_imaginary * twist_cosine + turned_real * twist_sine,
        ]
    )


def column_inverse(blocks, modulus):
    bin_rows = blocks.shape[2]
    half_rows = bin_rows // 2
    cosines, sine_values = phase_table(counting(half_rows), counting(bin_rows), bin_rows)
    summed = contract("ckr,jk->cjr", blocks[0], cosines) - contract(
        "ckr,jk->cjr", blocks[1], sine_values
    )
    return summed / modulus


def conjugate_product(left_side, right_side):
    real_part = left_side[0] * right_side[0] + left_side[1] * right_side[1]
    imaginary = left_side[1] * right_side[0] - left_side[0] * right_side[1]
    return jnp.stack([real_part, imaginary])


def gradient_spectra(spectrum, filters, inputs):
    input_part = conjugate_product(spectrum, filters)
    filter_part = conjugate_product(spectrum, inputs)
    return jnp.concatenate([input_part, filter_part], axis=1)


def on_device(grad_out, input_spectrum, filter_spectrum):
    channels = grad_out.shape[1]
    tokens_here = grad_out.shape[2]
    shards = lax.axis_size("seq")
    shard_index = lax.axis_index("seq")
    bin_columns = filter_spectrum.shape[3]
    row_block = filter_spectrum.shape[2]
    bin_rows = row_block * shards
    modulus = bin_rows * bin_columns
    time_rows = tokens_here // bin_columns
    signal = grad_out[0].reshape(channels, time_rows, bin_columns)
    groups = lax.axis_size("chan")
    group_index = lax.axis_index("chan")
    column_slice = bin_columns // (shards * groups)
    pieces = lax.all_to_all(signal[None], ("seq", "chan"), split_axis=3, concat_axis=0, tiled=True)
    columns = (
        pieces.reshape(shards, groups, channels, time_rows, column_slice)
        .transpose(1, 2, 0, 3, 4)
        .reshape(groups * channels, bin_rows // 2, column_slice)
    )
    mixed = column_forward(
        columns.astype(jnp.float32), (shard_index * groups + group_index) * column_slice, modulus
    )
    outgoing = (
        mixed.reshape(2, groups, channels, shards, row_block, column_slice)
        .transpose(3, 1, 0, 2, 4, 5)
        .reshape(shards * groups, 2, channels, row_block, column_slice)
    )
    spectrum = row_forward(
        lax.all_to_all(outgoing, ("seq", "chan"), split_axis=0, concat_axis=4, tiled=True)[0]
    )
    stacked = gradient_spectra(spectrum, filter_spectrum, input_spectrum[0])
    carried = stacked.shape[1]
    unwound = row_inverse(stacked, shard_index * row_block, modulus)
    arrived = lax.all_to_all(
        unwound[None], ("seq", "chan"), split_axis=4, concat_axis=0, tiled=True
    )
    gathered = (
        arrived.reshape(shards, groups, 2, carried, row_block, column_slice)
        .transpose(2, 1, 3, 0, 4, 5)
        .reshape(2, groups * carried, bin_rows, column_slice)
    )
    timeline = column_inverse(gathered, modulus)
    leaving = (
        timeline.reshape(groups, carried, shards, time_rows, column_slice)
        .transpose(2, 0, 1, 3, 4)
        .reshape(shards * groups, carried, time_rows, column_slice)
    )
    result = lax.all_to_all(leaving, ("seq", "chan"), split_axis=0, concat_axis=3, tiled=True)[0]
    input_grad = result[:channels].reshape(1, channels, tokens_here).astype(jnp.bfloat16)
    filter_rows = result[channels:]
    filter_full = filter_rows.reshape(channels, tokens_here)
    filter_grad = lax.psum_scatter(filter_full, "dp", scatter_dimension=1, tiled=True)
    return (input_grad, filter_grad)


def solution(mesh):
    in_specs = (
        P("dp", "chan", "seq"),
        P("dp", None, "chan", "seq", None),
        P(None, "chan", "seq", None),
    )
    out_specs = (P("dp", "chan", "seq"), P("chan", ("seq", "dp")))
    return jax.shard_map(
        on_device, mesh=mesh, in_specs=in_specs, out_specs=out_specs, check_vma=False
    )
```

profile of v0, /device:TPU:2, one launch (start us, length us, event | category | flops | bytes accessed | tf_op | source)
XLA Modules:
  0.0 470.5 jit_solution(423161714410286645)
XLA Ops:
  10.7 12.3 %all-to-all-start = ((bf16[64,2,1024]{2,1,0:T(2,128)(2,1)}), bf16[64,2,1024]{2,1,0:T(2,128)(2,1)S(1)}, u32[]{:S(2)}, u32[]{:S(2)}) async-start(bf16[64,2,1024]{2,1,0:T(2,128)(2,1)} %reshape.188), calls=%async_computation | async-start | bytes 524288 | tf_op jit(solution)/shard_map/all_to_all | solution.py:110
  23.2 11.9 %all-to-all-done = bf16[64,2,1024]{2,1,0:T(2,128)(2,1)S(1)} async-done(((bf16[64,2,1024]{2,1,0:T(2,128)(2,1)}), bf16[64,2,1024]{2,1,0:T(2,128)(2,1)S(1)}, u32[]{:S(2)}, u32[]{:S(2)}) %all-to-all-start) | async-done | bytes 262176 | tf_op jit(solution)/shard_map/all_to_all | solution.py:110
  40.4 3.7 add_bitcast_fusion.1
  52.7 5.5 %reshape.190 = f32[64,1,8192]{2,1,0:T(1,128)} reshape(f32[64,2,8,8,64]{4,3,2,1,0:T(8,128)} %bitcast.195) | data formatting | bytes 4194304
  58.1 5.7 %all-to-all-start.1 = ((f32[64,1,8192]{2,1,0:T(1,128)}), f32[64,1,8192]{2,1,0:T(1,128)S(1)}, u32[]{:S(2)}, u32[]{:S(2)}) async-start(f32[64,1,8192]{2,1,0:T(1,128)} %reshape.190), calls=%async_computation.1 | async-start | bytes 4194304 | tf_op jit(solution)/shard_map/all_to_all | solution.py:125
  64.7 50.4 %all-to-all-done.1 = f32[64,1,8192]{2,1,0:T(1,128)S(1)} async-done(((f32[64,1,8192]{2,1,0:T(1,128)}), f32[64,1,8192]{2,1,0:T(1,128)S(1)}, u32[]{:S(2)}, u32[]{:S(2)}) %all-to-all-start.1) | async-done | bytes 2097184 | tf_op jit(solution)/shard_map/all_to_all | solution.py:125
  116.9 7.5 %reduce = f32[64,8192]{1,0:T(8,128)S(1)} reduce(f32[64,1,8192]{2,1,0:T(1,128)} %copy-done.1, f32[]{:T(128)} %broadcast.291), dimensions={1}, to_apply=%all_to_all.47.reduce_sub_computation | reduce | bytes 4194308 | tf_op jit(solution)/shard_map/all_to_all | solution.py:125
  131.0 7.4 %fusion = f32[8,64,512]{2,1,0:T(8,128)S(1)} fusion(f32[1,1,8,64,64,8]{3,5,2,1,4,0:T(8,128)S(1)} %get-tuple-element.11), kind=kOutput, calls=%fused_computation.7 | convolution fusion | flops 1614282752 | bytes 2097152 | tf_op jit(solution)/shard_map/ckr,rq->ckq/dot_general | solution.py:22
  138.4 7.6 %fusion.2 = f32[8,64,512]{2,1,0:T(8,128)S(1)} fusion(f32[1,1,8,64,64,8]{3,5,2,1,4,0:T(8,128)S(1)} %get-tuple-element.11), kind=kOutput, calls=%fused_computation.9 | convolution fusion | flops 1614282752 | bytes 2097152 | tf_op jit(solution)/shard_map/ckr,rq->ckq/dot_general | solution.py:22
  146.0 7.4 %fusion.18 = f32[8,64,512]{2,1,0:T(8,128)S(1)} fusion(f32[8,64,512]{2,1,0:T(8,128)S(1)} %fusion.2, f32[1,1,8,64,64,8]{3,5,2,1,4,0:T(8,128)S(1)} %get-tuple-element.10), kind=kOutput, calls=%fused_computation.30 | convolution fusion | flops 1614544896 | bytes 3145728 | tf_op jit(solution)/shard_map/ckr,rq->ckq/dot_general | solution.py:22
  153.4 8.0 %fusion.34 = (f32[1,8,64,512]{3,2,1,0:T(8,128)S(1)}, f32[1,8,64,512]{3,2,1,0:T(8,128)S(1)}, f32[1,8,64,512]{3,2,1,0:T(8,128)S(1)}, f32[1,8,64,512]{3,2,1,0:T(8,128)S(1)}) fusion(f32[8,64,512]{2,1,0:T(8,128)S(1)} %fusion.18, f32[2,8,64,512]{3,2,1,0:T(8,128)S(1)} %copy-done.3, f32[1,2,8,64,512]{4,3,2,1,0:T(8,128)S(1)} %copy-done.4, ...), kind=kOutput, calls=%fused_computation.50 | convolution fusion | flops 1617690624 | bytes 11534336 | tf_op jit(solution)/shard_map/ckr,rq->ckq/dot_general | solution.py:22
  162.2 7.3 %fusion.8 = f32[16,64,512]{2,1,0:T(8,128)S(1)} fusion(f32[2,16,64,512]{3,2,1,0:T(8,128)S(1)} %maximum_maximum_fusion), kind=kOutput, calls=%fused_computation.17 | convolution fusion | flops 3224895488 | bytes 4194304 | tf_op jit(solution)/shard_map/ckr,rq->ckq/dot_general | solution.py:22
  169.5 7.7 %fusion.9 = f32[16,64,512]{2,1,0:T(8,128)S(1)} fusion(f32[2,16,64,512]{3,2,1,0:T(8,128)S(1)} %maximum_maximum_fusion), kind=kOutput, calls=%fused_computation.18 | convolution fusion | flops 3224895488 | bytes 4194304 | tf_op jit(solution)/shard_map/ckr,rq->ckq/dot_general | solution.py:22
  177.2 7.5 %fusion.16 = f32[16,64,512]{2,1,0:T(8,128)S(1)} fusion(f32[16,64,512]{2,1,0:T(8,128)S(1)} %fusion.9, f32[2,16,64,512]{3,2,1,0:T(8,128)S(1)} %maximum_maximum_fusion), kind=kOutput, calls=%fused_computation.25 | convolution fusion | flops 3225419776 | bytes 6291456 | tf_op jit(solution)/shard_map/ckr,rq->ckq/dot_general | solution.py:22
  184.8 7.9 %subtract_bitcast_fusion = (f32[1,16,64,512]{3,2,1,0:T(8,128)S(1)}, f32[1,16,64,512]{3,2,1,0:T(8,128)S(1)}) fusion(f32[16,64,512]{2,1,0:T(8,128)S(1)} %fusion.16, f32[64,512]{1,0:T(8,128)S(1)} %get-tuple-element.17, f32[64,512]{1,0:T(8,128)S(1)} %get-tuple-element.16, f32[16,64,512]{2,1,0:T(8,128)S(1)} %fusion.8, f32[2,16,64,512]{3,2,1,0:T(8,128)S(1)} %maximum_maximum_fusion), kind=kOutput, calls=%fused_computation.16 | convolution fusion | flops 3228565504 | bytes 10747904 | tf_op jit(solution)/shard_map/ckr,rq->ckq/dot_general | solution.py:22
  195.3 9.3 %copy.53 = f32[1,2,16,64,512]{3,2,1,0,4:T(8,128)} copy(f32[1,2,16,64,512]{4,3,2,1,0:T(8,128)} %maximum_bitcast_fusion) | data formatting | bytes 8388608 | tf_op jit(solution)/shard_map/broadcast_in_dim | solution.py:131
  204.6 9.7 %reshape.192 = f32[64,1,16384]{2,1,0:T(1,128)} reshape(f32[512,1,2,16,64]{4,3,2,1,0:T(8,128)} %bitcast.190) | data formatting | bytes 8388608
  214.3 101.8 %all_to_all.60 = f32[64,1,16384]{2,1,0:T(1,128)} all-to-all(f32[64,1,16384]{2,1,0:T(1,128)} %reshape.192), channel_id=1, replica_groups=mesh['seq'=8,'chan'=8,'dp'=4] {'seq','chan'}, dimensions={0} | all-to-all | bytes 8388608 | tf_op jit(solution)/shard_map/all_to_all | solution.py:130
  316.2 13.7 %reduce.1 = f32[64,16384]{1,0:T(8,128)} reduce(f32[64,1,16384]{2,1,0:T(1,128)} %all_to_all.60, f32[]{:T(128)} %broadcast.291), dimensions={1}, to_apply=%all_to_all.50.reduce_sub_computation | reduce | bytes 8388612 | tf_op jit(solution)/shard_map/all_to_all | solution.py:130
  329.9 7.4 %reshape.193 = f32[512,1,2,16,64]{4,3,2,1,0:T(8,128)} reshape(f32[64,16384]{1,0:T(8,128)} %reduce.1) | data formatting | bytes 8388608
  337.2 8.2 %copy.92 = f32[8,8,2,16,64,8]{4,0,3,1,5,2:T(8,128)S(1)} copy(f32[8,8,2,16,64,8]{4,3,2,5,1,0:T(8,128)} %bitcast.192) | data formatting | bytes 8388608 | tf_op jit(solution)/shard_map/reshape | solution.py:134
  345.5 3.8 fusion.140
  352.7 5.2 %squeeze.49 = f32[128,512,8]{1,0,2:T(8,128)} reshape(f32[1,8,16,8,64,8]{4,3,2,1,5,0:T(8,128)} %get-tuple-element.3) | data formatting | bytes 4194304 | tf_op jit(solution)/shard_map/squeeze | solution.py:78
  357.9 5.4 %fusion.53 = f32[256,128,8]{1,0,2:T(8,128)S(1)} fusion(f32[128,512,8]{1,0,2:T(8,128)} %squeeze.49), kind=kOutput, calls=%fused_computation.76 | convolution fusion | flops 1612447744 | bytes 3145728 | tf_op jit(solution)/shard_map/ckr,jk->cjr/dot_general | solution.py:22
  363.4 3.9 fusion.25
  370.2 5.0 %copy.57 = f32[8,8,16,32,8]{3,4,2,1,0:T(8,128)} copy(f32[8,8,16,32,8]{3,0,4,2,1:T(8,128)} %bitcast.193) | data formatting | bytes 2097152 | tf_op jit(solution)/shard_map/transpose | solution.py:141
  375.2 3.8 reshape.194
  379.0 34.2 %all_to_all.61 = f32[64,1,4096]{2,1,0:T(1,128)S(1)} all-to-all(f32[64,1,4096]{2,1,0:T(1,128)S(1)} %reshape.194), channel_id=1, replica_groups=mesh['seq'=8,'chan'=8,'dp'=4] {'seq','chan'}, dimensions={0} | all-to-all | bytes 2097152 | tf_op jit(solution)/shard_map/all_to_all | solution.py:144
  423.8 7.3 %copy.59 = f32[1,8,32,64,8]{4,3,2,1,0:T(8,128)} copy(f32[1,8,32,64,8]{2,4,1,3,0:T(8,128)S(1)} %slice.72) | data formatting | bytes 1048576 | tf_op jit(solution)/shard_map/slice | solution.py:146
  431.2 11.5 %reshape.183 = f32[8,16384]{1,0:T(8,128)} reshape(f32[1,8,32,64,8]{4,3,2,1,0:T(8,128)} %copy.59) | data formatting | bytes 1048576 | tf_op jit(solution)/shard_map/reshape | solution.py:147
  444.5 7.5 %copy.58 = bf16[1,8,32,64,8]{4,3,2,1,0:T(8,128)(2,1)} copy(bf16[1,8,32,64,8]{2,4,1,3,0:T(8,128)(2,1)S(1)} %slice.92) | data formatting | bytes 524288 | tf_op jit(solution)/shard_map/slice | solution.py:145
  452.0 11.1 %convert_element_type.65 = bf16[1,8,16384]{2,1,0:T(8,128)(2,1)} reshape(bf16[1,8,32,64,8]{4,3,2,1,0:T(8,128)(2,1)} %copy.58) | data formatting | bytes 524288 | tf_op jit(solution)/shard_map/convert_element_type | solution.py:145
  (43 shorter events, 49.0 us)
Async XLA Ops:
  10.7 24.4 %all-to-all-start = ((bf16[64,2,1024]{2,1,0:T(2,128)(2,1)}), bf16[64,2,1024]{2,1,0:T(2,128)(2,1)S(1)}, u32[]{:S(2)}, u32[]{:S(2)}) async-start(bf16[64,2,1024]{2,1,0:T(2,128)(2,1)} %reshape.188), calls=%async_computation | async-start | bytes 524288 | tf_op jit(solution)/shard_map/all_to_all | solution.py:110
  48.7 1.6 copy-start.2
  58.1 56.9 %all-to-all-start.1 = ((f32[64,1,8192]{2,1,0:T(1,128)}), f32[64,1,8192]{2,1,0:T(1,128)S(1)}, u32[]{:S(2)}, u32[]{:S(2)}) async-start(f32[64,1,8192]{2,1,0:T(1,128)} %reshape.190), calls=%async_computation.1 | async-start | bytes 4194304 | tf_op jit(solution)/shard_map/all_to_all | solution.py:125
  63.8 399.6 %reduce-scatter.2.cloned.1.call-start = ((), (), s32[]{:S(2)}) async-start(), calls=%async_computation.5 | async-start | bytes 655360 | tf_op jit(solution)/shard_map/reduce_scatter | solution.py:148
  115.1 1.3 copy-start.1
  146.0 7.4 %copy-start.3 = (f32[2,8,64,512]{3,2,1,0:T(8,128)S(1)}, f32[2,8,64,512]{3,2,1,0:T(8,128)}, u32[]{:S(2)}) copy-start(f32[2,8,64,512]{3,2,1,0:T(8,128)} %param.5) | copy-start | bytes 6291460
  146.0 7.4 %copy-start.4 = (f32[1,2,8,64,512]{4,3,2,1,0:T(8,128)S(1)}, f32[1,2,8,64,512]{4,3,2,1,0:T(8,128)}, u32[]{:S(2)}) copy-start(f32[1,2,8,64,512]{4,3,2,1,0:T(8,128)} %param.4) | copy-start | bytes 6291460
  421.6 2.0 copy-start
Sparse Core Ops, SparseCore 0:
  442.8 20.5 reduce-scatter.1
where the time goes:
time: 475 us; the launch traced here: 471 us
  blocking collectives  136 us (29%)
  local copies, waits for them, and re-layouts  131 us (28%)
  matrix products  76.9 us (16%)
  waiting for transfers between devices  62.7 us (13%)
  other arithmetic  30.9 us (7%)
  starting transfers between devices  18.2 us (4%)
  between operations  14.6 us (3%)
    all_to_all x1, blocking collectives, on_device(): lax.all_to_all(unwound[None], ('seq', 'chan'), split_axis=4, concat_axis=...  102 us
    dot_general x12, matrix products, contract(): jnp.einsum(pattern, left_side, right_side, precision=HIGHEST_PRECISION)  76.9 us
    all_to_all x1, waiting for transfers between devices, on_device(): lax.all_to_all(outgoing, ('seq', 'chan'), split_axis=0, concat_axis=4, ti...  50.4 us
    unnamed x19, local copies, waits for them, and re-layouts  39.4 us
    all_to_all x1, blocking collectives, on_device(): lax.all_to_all(leaving, ('seq', 'chan'), split_axis=0, concat_axis=3, til...  34.2 us
    all_to_all x1, other arithmetic, on_device(): lax.all_to_all(unwound[None], ('seq', 'chan'), split_axis=4, concat_axis=...  13.7 us
    all_to_all x1, starting transfers between devices, on_device(): lax.all_to_all(signal[None], ('seq', 'chan'), split_axis=3, concat_axis=0...  12.3 us
    all_to_all x1, waiting for transfers between devices, on_device(): lax.all_to_all(signal[None], ('seq', 'chan'), split_axis=3, concat_axis=0...  11.9 us
  transfers between devices with their start and end apart: 3, of which 3 were waited for; matrix products, arithmetic and copies ran while one was open for 4% of the time, Pallas kernels for 0%

commit v1 on v0

v1 whole, which is shorter than its diff:
```python
import functools

import jax
import jax.numpy as jnp
import numpy as np
from jax import lax
from jax.experimental import pallas as pl
from jax.experimental.pallas import tpu as pltpu
from jax.sharding import PartitionSpec as P

MESH = pl.DeviceIdType.MESH
F32 = jnp.float32
BF16 = jnp.bfloat16

SHARDS = 8
BATCHES = 4
CH = 8
HALF = 4
ROWS = 64
COLS = 512
BINS = 512
TIMES = 32
MODULUS = BINS * COLS


def split_table(table):
    high = table.astype(np.float32).astype(jnp.bfloat16)
    low = (table - high.astype(np.float64)).astype(np.float32).astype(jnp.bfloat16)
    return high, low


@functools.cache
def tables():
    turn = 2.0 * np.pi
    angle = turn * (np.outer(np.arange(COLS), np.arange(COLS)) % COLS) / COLS
    cos_high, cos_low = split_table(np.cos(angle))
    sin_high, sin_low = split_table(np.sin(angle))
    wide = np.concatenate(
        [
            np.concatenate([cos_high, cos_high, cos_low], axis=0),
            np.concatenate([sin_high, sin_high, sin_low], axis=0),
        ],
        axis=1,
    )
    half = BINS // 2
    time_angle = turn * (np.outer(np.arange(BINS), np.arange(half)) % BINS) / BINS
    cos_t = np.cos(time_angle).reshape(SHARDS, ROWS, half)
    sin_t = np.sin(time_angle).reshape(SHARDS, ROWS, half)
    first = np.concatenate([cos_t, -sin_t], axis=1)
    first_high, first_low = split_table(first)
    first_table = np.concatenate([first_high, first_low], axis=1)
    last = np.concatenate([cos_t, -sin_t], axis=1).transpose(0, 2, 1) / MODULUS
    last_high, last_low = split_table(last)
    last_table = np.concatenate([last_high, last_high, last_low], axis=2)
    twist = turn * np.outer(np.arange(BINS), np.arange(COLS)) / MODULUS
    twist_table = np.stack(
        [np.cos(twist).reshape(SHARDS, ROWS, COLS), np.sin(twist).reshape(SHARDS, ROWS, COLS)],
        axis=1,
    ).astype(np.float32)
    return wide, first_table, last_table, twist_table


def split(value):
    high = value.astype(BF16)
    low = (value - high.astype(F32)).astype(BF16)
    return high, low


def kernel(
    x_ref, xs_hbm, hs_hbm, wide_hbm, first_hbm, last_hbm, twist_hbm,
    in_ref, fl_ref,
    wide, first, last, twist, xs, hs, xf, xg, z3, d3, pcs, u, part, recv, dh, dh_recv,
    u_f, part_f, recv_f, back, load_sem, ag_send, ag_recv, rs_send, rs_recv, y_send, y_recv,
    f_send, f_recv, b_send, b_recv,
):
    me = lax.axis_index("seq")
    batch = lax.axis_index("dp")

    def ring(offset):
        return lax.rem(me + (offset + SHARDS), SHARDS)

    def peer(offset):
        return lax.rem(batch + offset, BATCHES)

    barrier = pltpu.get_barrier_semaphore()
    for offset in (1, -1):
        pl.semaphore_signal(barrier, inc=1, device_id={"seq": ring(offset)}, device_id_type=MESH)
    for offset in (1, 2, 3):
        pl.semaphore_signal(barrier, inc=1, device_id={"dp": peer(offset)}, device_id_type=MESH)

    loads = [
        pltpu.make_async_copy(first_hbm.at[me], first, load_sem.at[0]),
        pltpu.make_async_copy(twist_hbm.at[me], twist, load_sem.at[1]),
        pltpu.make_async_copy(wide_hbm, wide, load_sem.at[2]),
        pltpu.make_async_copy(hs_hbm, hs, load_sem.at[3]),
        pltpu.make_async_copy(xs_hbm.at[0], xs, load_sem.at[4]),
        pltpu.make_async_copy(last_hbm.at[me], last, load_sem.at[5]),
    ]
    for load in loads:
        load.start()

    def spread(j, carry):
        for n in range(4):
            lanes = pl.ds(pl.multiple_of(j * COLS + n * 128, 128), 128)
            xf[n, pl.ds(j, CH, stride=TIMES), :] = x_ref[0, :, lanes].astype(F32)
        return carry

    lax.fori_loop(0, TIMES, spread, 0)
    mine = pl.multiple_of(me * TIMES, TIMES)
    for c in range(CH):
        for n in range(4):
            value = xf[n, c * TIMES : (c + 1) * TIMES, :].astype(BF16)
            xg[c, pl.ds(mine, TIMES), n * 128 : (n + 1) * 128] = value

    pl.semaphore_wait(barrier, 5)

    long_way = (-1, -1, 1, 1)

    def gather_copy(q, k, long):
        way = long_way[q] if long else -long_way[q]
        source = pl.multiple_of(ring(-way * k) * TIMES, TIMES)
        block = xg.at[pl.ds(2 * q, 2), pl.ds(source, TIMES), :]
        slot = k if long else 4 + k
        return pltpu.make_async_remote_copy(
            src_ref=block, dst_ref=block, send_sem=ag_send.at[q, slot], recv_sem=ag_recv.at[q, slot],
            device_id={"seq": ring(way)}, device_id_type=MESH,
        )

    def gather_start(q):
        gather_copy(q, 0, True).start()
        gather_copy(q, 0, False).start()

    def gather_step(q, k):
        gather_copy(q, k, True).wait_recv()
        if k < 3:
            gather_copy(q, k + 1, True).start()
            gather_copy(q, k, False).wait_recv()
            if k < 2:
                gather_copy(q, k + 1, False).start()

    def stage_a(h):
        def body(c, carry):
            t = jnp.dot(first[...], xg[HALF * h + c], preferred_element_type=F32)
            real = t[0:64] + t[128:192]
            imag = t[64:128] + t[192:256]
            tc, ts = twist[0], twist[1]
            for index, value in enumerate((real * tc + imag * ts, imag * tc - real * ts)):
                high, low = split(value)
                rows = pl.ds(pl.multiple_of(index * HALF * ROWS + c * ROWS, ROWS), ROWS)
                z3[rows, 0:512] = high
                z3[rows, 512:1024] = low
                z3[rows, 1024:1536] = high
            return carry

        lax.fori_loop(0, HALF, body, 0)

    def columns(operand, rows, tiles):
        def body(n, carry):
            lanes = pl.ds(pl.multiple_of(n * 256, 256), 256)
            pcs[0:rows, lanes] = jnp.dot(
                operand[0:rows, :], wide[:, lanes], preferred_element_type=F32
            )
            return carry

        lax.fori_loop(tiles[0], tiles[1], body, 0)

    def products(h):
        def body(c, carry):
            rr = pl.ds(pl.multiple_of(c * ROWS, ROWS), ROWS)
            ri = pl.ds(pl.multiple_of(HALF * ROWS + c * ROWS, ROWS), ROWS)
            gr = pcs[rr, 0:512] + pcs[ri, 512:1024]
            gi = pcs[ri, 0:512] - pcs[rr, 512:1024]
            hr, hi = hs[0, HALF * h + c], hs[1, HALF * h + c]
            for rows, value in ((rr, gr * hr + gi * hi), (ri, gi * hr - gr * hi)):
                high, low = split(value)
                d3[rows, 0:512] = high
                d3[rows, 512:1024] = low
                d3[rows, 1024:1536] = high
            xr, xi = xs[0, HALF * h + c], xs[1, HALF * h + c]
            dh[h, c, 0] = gr * xr + gi * xi
            dh[h, c, 1] = gi * xr - gr * xi
            return carry

        lax.fori_loop(0, HALF, body, 0)

    def untwist(count, dest):
        def body(c, carry):
            rr = pl.ds(pl.multiple_of(c * ROWS, ROWS), ROWS)
            ri = pl.ds(pl.multiple_of(count * ROWS + c * ROWS, ROWS), ROWS)
            vr = pcs[rr, 0:512] - pcs[ri, 512:1024]
            vi = pcs[ri, 0:512] + pcs[rr, 512:1024]
            tc, ts = twist[0], twist[1]
            for index, value in enumerate((vr * tc - vi * ts, vi * tc + vr * ts)):
                high, low = split(value)
                dest[c, 64 * index : 64 * index + 64, :] = high
                dest[c, 128 + 64 * index : 192 + 64 * index, :] = low
                dest[c, 256 + 64 * index : 320 + 64 * index, :] = high
            return carry

        lax.fori_loop(0, count, body, 0)

    def stage_e(count, source, dest, base):
        def body(c, carry):
            y = jnp.dot(last[...], source[c], preferred_element_type=F32)
            dest[:, base + c] = y.reshape(SHARDS, TIMES, COLS)
            return carry

        lax.fori_loop(0, count, body, 0)

    def reduce_copy(bufs, piece, way, k, long):
        part_ref, recv_ref, send, received = bufs
        q, first_c, n_c = piece
        direction = way if long else -way
        hops = 4 if long else 3
        slot = k if long else 4 + k
        return pltpu.make_async_remote_copy(
            src_ref=part_ref.at[ring(direction * (hops - k)), pl.ds(first_c, n_c)],
            dst_ref=recv_ref.at[slot, pl.ds(first_c, n_c)],
            send_sem=send.at[q, slot], recv_sem=received.at[q, slot],
            device_id={"seq": ring(direction)}, device_id_type=MESH,
        )

    def reduce_start(bufs, piece, way):
        reduce_copy(bufs, piece, way, 0, True).start()
        reduce_copy(bufs, piece, way, 0, False).start()

    def reduce_half(bufs, piece, way, k, long):
        part_ref, recv_ref, _, _ = bufs
        _, first_c, n_c = piece
        hops = 4 if long else 3
        direction = way if long else -way
        slot = k if long else 4 + k
        reduce_copy(bufs, piece, way, k, long).wait_recv()
        if k < hops - 1:
            dest = ring(direction * (hops - 1 - k))
            for c in range(first_c, first_c + n_c):
                part_ref[dest, c] += recv_ref[slot, c]
            reduce_copy(bufs, piece, way, k + 1, long).start()

    def reduce_step(bufs, piece, way, k):
        reduce_half(bufs, piece, way, k, True)
        if k < 3:
            reduce_half(bufs, piece, way, k, False)

    big = (part, recv, rs_send, rs_recv)
    small = (part_f, recv_f, f_send, f_recv)

    def batch_copy(h, o):
        return pltpu.make_async_remote_copy(
            src_ref=dh.at[h, peer(o)], dst_ref=dh_recv.at[h, o - 1],
            send_sem=y_send.at[h, o - 1], recv_sem=y_recv.at[h, o - 1],
            device_id={"dp": peer(o)}, device_id_type=MESH,
        )

    for q in (0, 1):
        gather_start(q)
    for k in range(3):
        for q in (0, 1):
            gather_step(q, k)
    for q in (2, 3):
        gather_start(q)
    for q in (0, 1):
        gather_step(q, 3)

    loads[0].wait()
    loads[1].wait()
    stage_a(0)
    for q in (2, 3):
        gather_step(q, 0)
    loads[2].wait()
    columns(z3, 512, (0, 4))
    for q in (2, 3):
        gather_step(q, 1)
    loads[3].wait()
    loads[4].wait()
    products(0)
    for o in (1, 2, 3):
        batch_copy(0, o).start()
    for q in (2, 3):
        gather_step(q, 2)
    columns(d3, 512, (0, 4))
    for q in (2, 3):
        gather_step(q, 3)
    untwist(HALF, u)
    loads[5].wait()
    stage_e(HALF, u, part, 0)
    pieces = [(q, 2 * q, 2) for q in range(4)]
    for q in (0, 1):
        reduce_start(big, pieces[q], long_way[q])
    stage_a(1)
    columns(z3, 512, (0, 4))
    for q in (0, 1):
        reduce_step(big, pieces[q], long_way[q], 0)
    products(1)
    for o in (1, 2, 3):
        batch_copy(1, o).start()
    columns(d3, 512, (0, 4))
    for q in (0, 1):
        reduce_step(big, pieces[q], long_way[q], 1)
    untwist(HALF, u)
    stage_e(HALF, u, part, HALF)
    for q in (2, 3):
        reduce_start(big, pieces[q], long_way[q])
    for q in (0, 1):
        reduce_step(big, pieces[q], long_way[q], 2)
    for q in (0, 1):
        reduce_step(big, pieces[q], long_way[q], 3)
    for q in (2, 3):
        reduce_step(big, pieces[q], long_way[q], 0)

    for h in range(2):
        for o in (1, 2, 3):
            batch_copy(h, o).wait_recv()
        for index in range(2):
            value = (dh[h, batch, index] + dh_recv[h, 0, index]) + (
                dh_recv[h, 1, index] + dh_recv[h, 2, index]
            )
            high, low = split(value)
            rows = slice(index * 128 + h * 64, index * 128 + h * 64 + 64)
            z3[rows, 0:512] = high
            z3[rows, 512:1024] = low
            z3[rows, 1024:1536] = high
    for q in (2, 3):
        reduce_step(big, pieces[q], long_way[q], 1)
    columns(z3, 256, (0, 4))
    untwist(2, u_f)
    stage_e(2, u_f, part_f, 0)
    small_pieces = [(0, 0, 1), (1, 1, 1)]
    small_way = (-1, 1)
    for q in (0, 1):
        reduce_start(small, small_pieces[q], small_way[q])
    for k in range(4):
        if k < 2:
            for q in (2, 3):
                reduce_step(big, pieces[q], long_way[q], 2 + k)
        for q in (0, 1):
            reduce_step(small, small_pieces[q], small_way[q], k)

    def back_copy(h, o):
        there = pl.multiple_of(peer(o) * 8, 8)
        return pltpu.make_async_remote_copy(
            src_ref=part_f.at[me, h, pl.ds(there, 8), :],
            dst_ref=back.at[pl.ds(pl.multiple_of((HALF * h + batch) * 8, 8), 8), :],
            send_sem=b_send.at[h, o - 1], recv_sem=b_recv.at[h, o - 1],
            device_id={"dp": peer(o)}, device_id_type=MESH,
        )

    for h in range(2):
        part_f[me, h] += recv_f[3, h] + recv_f[6, h]
        for o in (1, 2, 3):
            back_copy(h, o).start()
        here = pl.multiple_of(batch * 8, 8)
        back[pl.ds(pl.multiple_of((HALF * h + batch) * 8, 8), 8), :] = part_f[
            me, h, pl.ds(here, 8), :
        ]

    for c in range(CH):
        value = part[me, c] + (recv[3, c] + recv[6, c])
        for n in range(4):
            xf[n, c * TIMES : (c + 1) * TIMES, :] = value[:, n * 128 : (n + 1) * 128]

    def collect(j, carry):
        for n in range(4):
            lanes = pl.ds(pl.multiple_of(j * COLS + n * 128, 128), 128)
            in_ref[0, :, lanes] = xf[n, pl.ds(j, CH, stride=TIMES), :].astype(BF16)
        return carry

    lax.fori_loop(0, TIMES, collect, 0)

    for h in range(2):
        for o in (1, 2, 3):
            back_copy(h, o).wait_recv()
    for n in range(4):
        xf[n, 0:64, :] = back[:, n * 128 : (n + 1) * 128]
        for j in range(8):
            start = j * COLS + n * 128
            fl_ref[:, start : start + 128] = xf[n, pl.ds(j, CH, stride=8), :]

    for q in range(4):
        for k in range(4):
            gather_copy(q, k, True).wait_send()
            reduce_copy(big, pieces[q], long_way[q], k, True).wait_send()
            if k < 3:
                gather_copy(q, k, False).wait_send()
                reduce_copy(big, pieces[q], long_way[q], k, False).wait_send()
    for q in range(2):
        for k in range(4):
            reduce_copy(small, small_pieces[q], small_way[q], k, True).wait_send()
            if k < 3:
                reduce_copy(small, small_pieces[q], small_way[q], k, False).wait_send()
        for o in (1, 2, 3):
            batch_copy(q, o).wait_send()
            back_copy(q, o).wait_send()


def on_device(grad_out, input_spectrum, filter_spectrum):
    wide, first, last, twist = (jnp.asarray(t) for t in tables())
    vmem = pl.BlockSpec(memory_space=pltpu.VMEM)
    anywhere = pl.BlockSpec(memory_space=pl.ANY)
    dma = pltpu.SemaphoreType.DMA
    return pl.pallas_call(
        kernel,
        out_shape=(
            jax.ShapeDtypeStruct((1, CH, TIMES * COLS), BF16),
            jax.ShapeDtypeStruct((CH, TIMES * COLS // BATCHES), F32),
        ),
        in_specs=[vmem] + [anywhere] * 6,
        out_specs=(vmem, vmem),
        scratch_shapes=[
            pltpu.VMEM((1536, 1024), BF16),
            pltpu.VMEM((256, 256), BF16),
            pltpu.VMEM((256, 384), BF16),
            pltpu.VMEM((2, ROWS, COLS), F32),
            pltpu.VMEM((2, CH, ROWS, COLS), F32),
            pltpu.VMEM((2, CH, ROWS, COLS), F32),
            pltpu.VMEM((4, CH * TIMES, 128), F32),
            pltpu.VMEM((CH, SHARDS * TIMES, COLS), BF16),
            pltpu.VMEM((512, 1536), BF16),
            pltpu.VMEM((512, 1536), BF16),
            pltpu.VMEM((512, 1024), F32),
            pltpu.VMEM((HALF, 384, COLS), BF16),
            pltpu.VMEM((SHARDS, CH, TIMES, COLS), F32),
            pltpu.VMEM((7, CH, TIMES, COLS), F32),
            pltpu.VMEM((2, BATCHES, 2, ROWS, COLS), F32),
            pltpu.VMEM((2, 3, 2, ROWS, COLS), F32),
            pltpu.VMEM((2, 384, COLS), BF16),
            pltpu.VMEM((SHARDS, 2, TIMES, COLS), F32),
            pltpu.VMEM((7, 2, TIMES, COLS), F32),
            pltpu.VMEM((CH * 8, COLS), F32),
            dma((6,)),
            dma((4, 7)), dma((4, 7)),
            dma((4, 7)), dma((4, 7)),
            dma((2, 3)), dma((2, 3)),
            dma((2, 7)), dma((2, 7)),
            dma((2, 3)), dma((2, 3)),
        ],
        compiler_params=pltpu.CompilerParams(
            collective_id=0, has_side_effects=True, vmem_limit_bytes=56 * 1024 * 1024
        ),
    )(grad_out, input_spectrum, filter_spectrum, wide, first, last, twist)


def solution(mesh):
    in_specs = (
        P("dp", "chan", "seq"),
        P("dp", None, "chan", "seq", None),
        P(None, "chan", "seq", None),
    )
    out_specs = (P("dp", "chan", "seq"), P("chan", ("seq", "dp")))
    return jax.shard_map(
        on_device, mesh=mesh, in_specs=in_specs, out_specs=out_specs, check_vma=False
    )
```

time: 475 us -> 107 us (0.23)
  blocking collectives: 136 us -> 0 us
  local copies, waits for them, and re-layouts: 131 us -> 3.24 us
  Pallas kernels: 0 us -> 103 us
  matrix products: 76.9 us -> 0 us
  waiting for transfers between devices: 62.7 us -> 0 us
  other arithmetic: 30.9 us -> 0 us
  starting transfers between devices: 18.2 us -> 0 us
  between operations: 14.6 us -> 0.64 us
    all_to_all x2 -> x0, blocking collectives: 136 us -> none  [the longest x1 102 us: on_device(): lax.all_to_all(unwound[None], ('seq', 'chan'), split_axis=4, concat_axis=...]
    pallas_call x0 -> x1, Pallas kernels: none -> 103 us  [on_device(): pl.pallas_call(kernel, out_shape=(jax.ShapeDtypeStruct((1, CH, TIMES * CO...]
    dot_general x12 -> x0, matrix products: 76.9 us -> none  [contract(): jnp.einsum(pattern, left_side, right_side, precision=HIGHEST_PRECISION)]
    all_to_all x2 -> x0, waiting for transfers between devices: 62.3 us -> none  [the longest x1 50.4 us: on_device(): lax.all_to_all(outgoing, ('seq', 'chan'), split_axis=0, concat_axis=4, ti...]
    unnamed x19 -> x2, local copies, waits for them, and re-layouts: 39.4 us -> 3.24 us
    all_to_all x3 -> x0, other arithmetic: 24.5 us -> none  [the longest x1 13.7 us: on_device(): lax.all_to_all(unwound[None], ('seq', 'chan'), split_axis=4, concat_axis=...]
    reshape x4 -> x0, local copies, waits for them, and re-layouts: 22.9 us -> none  [the longest x1 11.5 us: on_device(): filter_full = filter_rows.reshape(channels, tokens_here)]
    slice x6 -> x0, local copies, waits for them, and re-layouts: 21.1 us -> none  [the longest x2 9.25 us: on_device(): result[:channels].reshape(1, channels, tokens_here).astype(jnp.bfloat16)]
  transfers between devices with their start and end apart: 3 -> 0, of which waited for: 3 -> 0; matrix products, arithmetic and copies ran while one was open for 4% -> 0% of each run, Pallas kernels for 0% -> 0%
where the time goes in v1:
time: 107 us
  Pallas kernels  103 us (96%)
  local copies, waits for them, and re-layouts  3.24 us (3%)
    pallas_call x1, Pallas kernels, on_device(): pl.pallas_call(kernel, out_shape=(jax.ShapeDtypeStruct((1, CH, TIMES * CO...  103 us
    unnamed x2, local copies, waits for them, and re-layouts  3.24 us

profile of v1, /device:TPU:2, one launch (start us, length us, event | category | flops | bytes accessed | tf_op | source)
XLA Modules:
  0.0 106.8 jit_solution(16046246828660366066)
XLA Ops:
  0.6 102.9 %shard_map.86 = (bf16[1,8,16384]{2,1,0:T(8,128)(2,1)}, f32[8,4096]{1,0:T(8,128)}) custom-call(bf16[1,8,16384]{2,1,0:T(8,128)(2,1)} %x_ref.1, f32[1,2,8,64,512]{4,3,2,1,0:T(8,128)} %xs_hbm.1, f32[2,8,64,512]{3,2,1,0:T(8,128)} %hs_hbm.1, bf16[1536,1024]{1,0:T(8,128)(2,1)} %constant.8.clone.wide_hbm, bf16[8,256,256]{2,1,0:T(8,128)(2,1)} %constant.9.clone.first_hbm, ...), custom_call_target="tpu_custom_call" | custom-call | tf_op jit(solution)/shard_map/pallas_call | solution.py:401
  103.5 1.7 %copy.11 = bf16[1,8,16384]{2,1,0:T(8,128)(2,1)} copy(bf16[1,8,16384]{2,1,0:T(8,128)(2,1)} %get-tuple-element.4) | data formatting | bytes 524288
  105.2 1.6 %copy.12 = f32[8,4096]{1,0:T(8,128)} copy(f32[8,4096]{1,0:T(8,128)} %get-tuple-element.5) | data formatting | bytes 262144

commit v2 on v1

--- a/solution.py
+++ b/solution.py
@@ -60,6 +60,37 @@
     return wide, first_table, last_table, twist_table
 
 
+SPAN = 124.0
+GAIN = 2.0 ** (2.0 * SPAN / 32.0) - 1.0
+FLOOR = 2.0 ** (-SPAN / 32.0)
+
+
+def encode(values, put, put_top):
+    top = jnp.abs(values[0])
+    for value in values[1:]:
+        top = jnp.maximum(top, jnp.abs(value))
+    top = (jnp.maximum(top, 1e-30) * 1.01).astype(BF16)
+    put_top(top)
+    slope = (GAIN * FLOOR) / top.astype(F32)
+    for index, value in enumerate(values):
+        level = jnp.abs(value) * slope + FLOOR
+        for _ in range(5):
+            level = level * level
+        put(index, jnp.where(value < 0.0, -level, level).astype(BF16))
+
+
+def decode(codes, top):
+    unit = top.astype(F32) * (1.0 / GAIN)
+    slope = unit * (1.0 / FLOOR)
+    values = []
+    for code in codes:
+        wide_code = code.astype(F32)
+        level = jnp.exp2(jnp.log2(jnp.abs(wide_code)) * (1.0 / 32.0))
+        value = level * slope - unit
+        values.append(jnp.where(wide_code < 0.0, -value, value))
+    return values
+
+
 def split(value):
     high = value.astype(BF16)
     low = (value - high.astype(F32)).astype(BF16)
@@ -70,7 +101,7 @@
     x_ref, xs_hbm, hs_hbm, wide_hbm, first_hbm, last_hbm, twist_hbm,
     in_ref, fl_ref,
     wide, first, last, twist, xs, hs, xf, xg, z3, d3, pcs, u, part, recv, dh, dh_recv,
-    u_f, part_f, recv_f, back, load_sem, ag_send, ag_recv, rs_send, rs_recv, y_send, y_recv,
+    u_f, part_f, recv_f, back, sent, sent_f, load_sem, ag_send, ag_recv, rs_send, rs_recv, y_send, y_recv,
     f_send, f_recv, b_send, b_recv,
 ):
     me = lax.axis_index("seq")
@@ -114,7 +145,7 @@
 
     pl.semaphore_wait(barrier, 5)
 
-    long_way = (-1, -1, 1, 1)
+    long_way = (-1, 1, -1, 1)
 
     def gather_copy(q, k, long):
         way = long_way[q] if long else -long_way[q]
@@ -138,7 +169,7 @@
             if k < 2:
                 gather_copy(q, k + 1, False).start()
 
-    def stage_a(h):
+    def stage_a(h, lo, hi):
         def body(c, carry):
             t = jnp.dot(first[...], xg[HALF * h + c], preferred_element_type=F32)
             real = t[0:64] + t[128:192]
@@ -152,9 +183,9 @@
                 z3[rows, 1024:1536] = high
             return carry
 
-        lax.fori_loop(0, HALF, body, 0)
-
-    def columns(operand, rows, tiles):
+        lax.fori_loop(lo, hi, body, 0)
+
+    def columns(operand, rows, lo, hi):
         def body(n, carry):
             lanes = pl.ds(pl.multiple_of(n * 256, 256), 256)
             pcs[0:rows, lanes] = jnp.dot(
@@ -162,9 +193,9 @@
             )
             return carry
 
-        lax.fori_loop(tiles[0], tiles[1], body, 0)
-
-    def products(h):
+        lax.fori_loop(lo, hi, body, 0)
+
+    def products(h, lo, hi):
         def body(c, carry):
             rr = pl.ds(pl.multiple_of(c * ROWS, ROWS), ROWS)
             ri = pl.ds(pl.multiple_of(HALF * ROWS + c * ROWS, ROWS), ROWS)
@@ -181,9 +212,9 @@
             dh[h, c, 1] = gi * xr - gr * xi
             return carry
 
-        lax.fori_loop(0, HALF, body, 0)
-
-    def untwist(count, dest):
+        lax.fori_loop(lo, hi, body, 0)
+
+    def untwist(count, dest, lo, hi):
         def body(c, carry):
             rr = pl.ds(pl.multiple_of(c * ROWS, ROWS), ROWS)
             ri = pl.ds(pl.multiple_of(count * ROWS + c * ROWS, ROWS), ROWS)
@@ -197,53 +228,87 @@
                 dest[c, 256 + 64 * index : 320 + 64 * index, :] = high
             return carry
 
-        lax.fori_loop(0, count, body, 0)
-
-    def stage_e(count, source, dest, base):
+        lax.fori_loop(lo, hi, body, 0)
+
+    def stage_e(source, dest, base, lo, hi):
         def body(c, carry):
             y = jnp.dot(last[...], source[c], preferred_element_type=F32)
             dest[:, base + c] = y.reshape(SHARDS, TIMES, COLS)
             return carry
 
-        lax.fori_loop(0, count, body, 0)
-
-    def reduce_copy(bufs, piece, way, k, long):
-        part_ref, recv_ref, send, received = bufs
-        q, first_c, n_c = piece
-        direction = way if long else -way
+        lax.fori_loop(lo, hi, body, 0)
+
+    def reduce_copy(bufs, q, way, k, long):
+        _, sent_ref, recv_ref, send, received, _ = bufs
+        slot = k if long else 4 + k
+        return pltpu.make_async_remote_copy(
+            src_ref=sent_ref.at[q, slot], dst_ref=recv_ref.at[q, slot],
+            send_sem=send.at[q, slot], recv_sem=received.at[q, slot],
+            device_id={"seq": ring(way if long else -way)}, device_id_type=MESH,
+        )
+
+    def blocks(bufs, q):
+        n_c = bufs[5]
+        return [
+            (n_c * q + c, pl.ds(16 * r, 16), pl.ds(128 * n, 128))
+            for c in range(n_c)
+            for r in range(TIMES // 16)
+            for n in range(COLS // 128)
+        ]
+
+    def arrived(bufs, q, slot):
+        recv_ref = bufs[2]
+        count = len(blocks(bufs, q))
+        return decode([recv_ref[q, slot, b] for b in range(count)], recv_ref[q, slot, count])
+
+    def reduce_send(bufs, q, way, k, long, values):
+        sent_ref = bufs[1]
+        slot = k if long else 4 + k
+
+        def put(index, code):
+            sent_ref[q, slot, index] = code
+
+        def put_top(top):
+            sent_ref[q, slot, len(values)] = top
+
+        encode(values, put, put_top)
+        reduce_copy(bufs, q, way, k, long).start()
+
+    def reduce_hop(bufs, q, way, k, long):
+        part_ref = bufs[0]
         hops = 4 if long else 3
         slot = k if long else 4 + k
-        return pltpu.make_async_remote_copy(
-            src_ref=part_ref.at[ring(direction * (hops - k)), pl.ds(first_c, n_c)],
-            dst_ref=recv_ref.at[slot, pl.ds(first_c, n_c)],
-            send_sem=send.at[q, slot], recv_sem=received.at[q, slot],
-            device_id={"seq": ring(direction)}, device_id_type=MESH,
-        )
-
-    def reduce_start(bufs, piece, way):
-        reduce_copy(bufs, piece, way, 0, True).start()
-        reduce_copy(bufs, piece, way, 0, False).start()
-
-    def reduce_half(bufs, piece, way, k, long):
-        part_ref, recv_ref, _, _ = bufs
-        _, first_c, n_c = piece
-        hops = 4 if long else 3
-        direction = way if long else -way
-        slot = k if long else 4 + k
-        reduce_copy(bufs, piece, way, k, long).wait_recv()
-        if k < hops - 1:
-            dest = ring(direction * (hops - 1 - k))
-            for c in range(first_c, first_c + n_c):
-                part_ref[dest, c] += recv_ref[slot, c]
-            reduce_copy(bufs, piece, way, k + 1, long).start()
-
-    def reduce_step(bufs, piece, way, k):
-        reduce_half(bufs, piece, way, k, True)
+        dest = ring((way if long else -way) * (hops - 1 - k))
+        if k >= 0:
+            reduce_copy(bufs, q, way, k, long).wait_recv()
+        if k == hops - 1:
+            return
+        values = [part_ref[dest, c, rows, lanes] for c, rows, lanes in blocks(bufs, q)]
+        if k >= 0:
+            values = [a + b for a, b in zip(values, arrived(bufs, q, slot))]
+        reduce_send(bufs, q, way, k + 1, long, values)
+
+    def reduce_start(bufs, q, way):
+        reduce_hop(bufs, q, way, -1, True)
+        reduce_hop(bufs, q, way, -1, False)
+
+    def reduce_step(bufs, q, way, k):
+        reduce_hop(bufs, q, way, k, True)
         if k < 3:
-            reduce_half(bufs, piece, way, k, False)
-
-    big = (part, recv, rs_send, rs_recv)
-    small = (part_f, recv_f, f_send, f_recv)
+            reduce_hop(bufs, q, way, k, False)
+
+    def reduce_end(bufs, q):
+        part_ref = bufs[0]
+        return [
+            (c, rows, lanes, part_ref[me, c, rows, lanes] + (a + b))
+            for (c, rows, lanes), a, b in zip(
+                blocks(bufs, q), arrived(bufs, q, 3), arrived(bufs, q, 6)
+            )
+        ]
+
+    big = (part, sent, recv, rs_send, rs_recv, 2)
+    small = (part_f, sent_f, recv_f, f_send, f_recv, 1)
+    small_way = (-1, 1)
 
     def batch_copy(h, o):
         return pltpu.make_async_remote_copy(
@@ -251,6 +316,51 @@
             send_sem=y_send.at[h, o - 1], recv_sem=y_recv.at[h, o - 1],
             device_id={"dp": peer(o)}, device_id_type=MESH,
         )
+
+    def half_parts(h):
+        def start_pieces(q):
+            reduce_start(big, q, long_way[q])
+
+        def batch_starts():
+            for o in (1, 2, 3):
+                batch_copy(h, o).start()
+
+        def wait(index):
+            if h == 0:
+                loads[index].wait()
+
+        return [
+            lambda: (wait(0), wait(1), stage_a(h, 0, 2)),
+            lambda: stage_a(h, 2, 4),
+            lambda: (wait(2), columns(z3, 512, 0, 2)),
+            lambda: columns(z3, 512, 2, 4),
+            lambda: (wait(3), wait(4), products(h, 0, 2)),
+            lambda: (products(h, 2, 4), batch_starts()),
+            lambda: columns(d3, 512, 0, 2),
+            lambda: columns(d3, 512, 2, 4),
+            lambda: untwist(HALF, u, 0, 2),
+            lambda: untwist(HALF, u, 2, 4),
+            lambda: (wait(5), stage_e(u, part, HALF * h, 0, 2), start_pieces(2 * h)),
+            lambda: (stage_e(u, part, HALF * h, 2, 4), start_pieces(2 * h + 1)),
+        ]
+
+    def weave(parts, services):
+        done = 0
+        for index, part_of in enumerate(parts):
+            part_of()
+            while done * len(parts) < (index + 1) * len(services):
+                services[done]()
+                done += 1
+
+    def gather_services(pieces):
+        return [functools.partial(gather_step, q, k) for k in range(4) for q in pieces]
+
+    def reduce_services(bufs, pieces, ways, first=0):
+        return [
+            functools.partial(reduce_step, bufs, q, ways[q], k)
+            for k in range(first, 4)
+            for q in pieces
+        ]
 
     for q in (0, 1):
         gather_start(q)
@@ -261,54 +371,10 @@
         gather_start(q)
     for q in (0, 1):
         gather_step(q, 3)
-
-    loads[0].wait()
-    loads[1].wait()
-    stage_a(0)
-    for q in (2, 3):
-        gather_step(q, 0)
-    loads[2].wait()
-    columns(z3, 512, (0, 4))
-    for q in (2, 3):
-        gather_step(q, 1)
-    loads[3].wait()
-    loads[4].wait()
-    products(0)
-    for o in (1, 2, 3):
-        batch_copy(0, o).start()
-    for q in (2, 3):
-        gather_step(q, 2)
-    columns(d3, 512, (0, 4))
-    for q in (2, 3):
-        gather_step(q, 3)
-    untwist(HALF, u)
-    loads[5].wait()
-    stage_e(HALF, u, part, 0)
-    pieces = [(q, 2 * q, 2) for q in range(4)]
-    for q in (0, 1):
-        reduce_start(big, pieces[q], long_way[q])
-    stage_a(1)
-    columns(z3, 512, (0, 4))
-    for q in (0, 1):
-        reduce_step(big, pieces[q], long_way[q], 0)
-    products(1)
-    for o in (1, 2, 3):
-        batch_copy(1, o).start()
-    columns(d3, 512, (0, 4))
-    for q in (0, 1):
-        reduce_step(big, pieces[q], long_way[q], 1)
-    untwist(HALF, u)
-    stage_e(HALF, u, part, HALF)
-    for q in (2, 3):
-        reduce_start(big, pieces[q], long_way[q])
-    for q in (0, 1):
-        reduce_step(big, pieces[q], long_way[q], 2)
-    for q in (0, 1):
-        reduce_step(big, pieces[q], long_way[q], 3)
-    for q in (2, 3):
-        reduce_step(big, pieces[q], long_way[q], 0)
-
-    for h in range(2):
+    weave(half_parts(0), gather_services((2, 3)))
+    weave(half_parts(1), reduce_services(big, (0, 1), long_way))
+
+    def batch_sum(h):
         for o in (1, 2, 3):
             batch_copy(h, o).wait_recv()
         for index in range(2):
@@ -320,21 +386,26 @@
             z3[rows, 0:512] = high
             z3[rows, 512:1024] = low
             z3[rows, 1024:1536] = high
-    for q in (2, 3):
-        reduce_step(big, pieces[q], long_way[q], 1)
-    columns(z3, 256, (0, 4))
-    untwist(2, u_f)
-    stage_e(2, u_f, part_f, 0)
-    small_pieces = [(0, 0, 1), (1, 1, 1)]
-    small_way = (-1, 1)
-    for q in (0, 1):
-        reduce_start(small, small_pieces[q], small_way[q])
-    for k in range(4):
-        if k < 2:
-            for q in (2, 3):
-                reduce_step(big, pieces[q], long_way[q], 2 + k)
-        for q in (0, 1):
-            reduce_step(small, small_pieces[q], small_way[q], k)
+
+    filter_parts = [
+        lambda: batch_sum(0),
+        lambda: batch_sum(1),
+        lambda: columns(z3, 256, 0, 4),
+        lambda: (
+            untwist(2, u_f, 0, 2),
+            stage_e(u_f, part_f, 0, 0, 2),
+            reduce_start(small, 0, small_way[0]),
+            reduce_start(small, 1, small_way[1]),
+        ),
+    ]
+    services = reduce_services(big, (2, 3), long_way)
+    weave(filter_parts, services[:4])
+    small_services = reduce_services(small, (0, 1), small_way)
+    for index in range(4):
+        services[4 + index]()
+        small_services[index]()
+    for service in small_services[4:]:
+        service()
 
     def back_copy(h, o):
         there = pl.multiple_of(peer(o) * 8, 8)
@@ -346,7 +417,8 @@
         )
 
     for h in range(2):
-        part_f[me, h] += recv_f[3, h] + recv_f[6, h]
+        for c, rows, lanes, value in reduce_end(small, h):
+            part_f[me, c, rows, lanes] = value
         for o in (1, 2, 3):
             back_copy(h, o).start()
         here = pl.multiple_of(batch * 8, 8)
@@ -354,10 +426,9 @@
             me, h, pl.ds(here, 8), :
         ]
 
-    for c in range(CH):
-        value = part[me, c] + (recv[3, c] + recv[6, c])
-        for n in range(4):
-            xf[n, c * TIMES : (c + 1) * TIMES, :] = value[:, n * 128 : (n + 1) * 128]
+    for q in range(4):
+        for c, rows, lanes, value in reduce_end(big, q):
+            xf[lanes.start // 128, c * TIMES + rows.start : c * TIMES + rows.start + 16, :] = value
 
     def collect(j, carry):
         for n in range(4):
@@ -379,15 +450,15 @@
     for q in range(4):
         for k in range(4):
             gather_copy(q, k, True).wait_send()
-            reduce_copy(big, pieces[q], long_way[q], k, True).wait_send()
+            reduce_copy(big, q, long_way[q], k, True).wait_send()
             if k < 3:
                 gather_copy(q, k, False).wait_send()
-                reduce_copy(big, pieces[q], long_way[q], k, False).wait_send()
+                reduce_copy(big, q, long_way[q], k, False).wait_send()
     for q in range(2):
         for k in range(4):
-            reduce_copy(small, small_pieces[q], small_way[q], k, True).wait_send()
+            reduce_copy(small, q, small_way[q], k, True).wait_send()
             if k < 3:
-                reduce_copy(small, small_pieces[q], small_way[q], k, False).wait_send()
+                reduce_copy(small, q, small_way[q], k, False).wait_send()
         for o in (1, 2, 3):
             batch_copy(q, o).wait_send()
             back_copy(q, o).wait_send()
@@ -420,13 +491,15 @@
             pltpu.VMEM((512, 1024), F32),
             pltpu.VMEM((HALF, 384, COLS), BF16),
             pltpu.VMEM((SHARDS, CH, TIMES, COLS), F32),
-            pltpu.VMEM((7, CH, TIMES, COLS), F32),
+            pltpu.VMEM((4, 7, 17, 16, 128), BF16),
             pltpu.VMEM((2, BATCHES, 2, ROWS, COLS), F32),
             pltpu.VMEM((2, 3, 2, ROWS, COLS), F32),
             pltpu.VMEM((2, 384, COLS), BF16),
             pltpu.VMEM((SHARDS, 2, TIMES, COLS), F32),
-            pltpu.VMEM((7, 2, TIMES, COLS), F32),
+            pltpu.VMEM((2, 7, 9, 16, 128), BF16),
             pltpu.VMEM((CH * 8, COLS), F32),
+            pltpu.VMEM((4, 7, 17, 16, 128), BF16),
+            pltpu.VMEM((2, 7, 9, 16, 128), BF16),
             dma((6,)),
             dma((4, 7)), dma((4, 7)),
             dma((4, 7)), dma((4, 7)),

time: 107 us -> 91.6 us (0.86)
  Pallas kernels: 103 us -> 87.6 us
    pallas_call x1, Pallas kernels: 103 us -> 87.6 us  [on_device(): pl.pallas_call(kernel, out_shape=(jax.ShapeDtypeStruct((1, CH, TIMES * CO...]
where the time goes in v2:
time: 91.6 us; the launch traced here: 91.5 us
  Pallas kernels  87.6 us (96%)
  local copies, waits for them, and re-layouts  3.24 us (4%)
    pallas_call x1, Pallas kernels, on_device(): pl.pallas_call(kernel, out_shape=(jax.ShapeDtypeStruct((1, CH, TIMES * CO...  87.6 us
    unnamed x2, local copies, waits for them, and re-layouts  3.24 us

profile of v2, /device:TPU:2, one launch (start us, length us, event | category | flops | bytes accessed | tf_op | source)
XLA Modules:
  0.0 91.5 jit_solution(13032576941530949845)
XLA Ops:
  0.6 87.6 %shard_map.86 = (bf16[1,8,16384]{2,1,0:T(8,128)(2,1)}, f32[8,4096]{1,0:T(8,128)}) custom-call(bf16[1,8,16384]{2,1,0:T(8,128)(2,1)} %x_ref.1, f32[1,2,8,64,512]{4,3,2,1,0:T(8,128)} %xs_hbm.1, f32[2,8,64,512]{3,2,1,0:T(8,128)} %hs_hbm.1, bf16[1536,1024]{1,0:T(8,128)(2,1)} %constant.8.clone.wide_hbm, bf16[8,256,256]{2,1,0:T(8,128)(2,1)} %constant.9.clone.first_hbm, ...), custom_call_target="tpu_custom_call" | custom-call | tf_op jit(solution)/shard_map/pallas_call | solution.py:472
  88.2 1.7 %copy.11 = bf16[1,8,16384]{2,1,0:T(8,128)(2,1)} copy(bf16[1,8,16384]{2,1,0:T(8,128)(2,1)} %get-tuple-element.4) | data formatting | bytes 524288
  89.9 1.6 %copy.12 = f32[8,4096]{1,0:T(8,128)} copy(f32[8,4096]{1,0:T(8,128)} %get-tuple-element.5) | data formatting | bytes 262144

commit v3 on v2

--- a/solution.py
+++ b/solution.py
@@ -21,6 +21,7 @@
 BINS = 512
 TIMES = 32
 MODULUS = BINS * COLS
+LANES = 128
 
 
 def split_table(table):
@@ -32,16 +33,23 @@
 @functools.cache
 def tables():
     turn = 2.0 * np.pi
-    angle = turn * (np.outer(np.arange(COLS), np.arange(COLS)) % COLS) / COLS
-    cos_high, cos_low = split_table(np.cos(angle))
-    sin_high, sin_low = split_table(np.sin(angle))
-    wide = np.concatenate(
-        [
-            np.concatenate([cos_high, cos_high, cos_low], axis=0),
-            np.concatenate([sin_high, sin_high, sin_low], axis=0),
-        ],
-        axis=1,
-    )
+    fold = np.arange(LANES)
+    forward, inverse = [], []
+    for a in range(4):
+        angle = turn * (np.outer(4 * fold + a, fold) % COLS) / COLS
+        c, s = np.cos(angle), np.sin(angle)
+        for group, block in (
+            (forward, np.block([[c, -s], [s, c]])),
+            (inverse, np.block([[c.T, s.T], [-s.T, c.T]])),
+        ):
+            high, low = split_table(block)
+            group.append(np.concatenate([high, high, low], axis=0))
+    wide = np.stack(forward + inverse)
+    place = np.arange(COLS)
+    order = 4 * (place % LANES) + place // LANES
+    shuffle = np.zeros((COLS, COLS), np.float32)
+    shuffle[order, place] = 1.0
+    shuffle = np.stack([shuffle, shuffle.T]).astype(jnp.bfloat16)
     half = BINS // 2
     time_angle = turn * (np.outer(np.arange(BINS), np.arange(half)) % BINS) / BINS
     cos_t = np.cos(time_angle).reshape(SHARDS, ROWS, half)
@@ -56,8 +64,8 @@
     twist_table = np.stack(
         [np.cos(twist).reshape(SHARDS, ROWS, COLS), np.sin(twist).reshape(SHARDS, ROWS, COLS)],
         axis=1,
-    ).astype(np.float32)
-    return wide, first_table, last_table, twist_table
+    ).astype(np.float32)[..., order]
+    return wide, first_table, last_table, twist_table, shuffle
 
 
 SPAN = 124.0
@@ -98,10 +106,10 @@
 
 
 def kernel(
-    x_ref, xs_hbm, hs_hbm, wide_hbm, first_hbm, last_hbm, twist_hbm,
+    x_ref, xs_hbm, hs_hbm, wide_hbm, first_hbm, last_hbm, twist_hbm, shuffle_hbm,
     in_ref, fl_ref,
-    wide, first, last, twist, xs, hs, xf, xg, z3, d3, pcs, u, part, recv, dh, dh_recv,
-    u_f, part_f, recv_f, back, sent, sent_f, load_sem, ag_send, ag_recv, rs_send, rs_recv, y_send, y_recv,
+    wide, first, last, twist, shuffle, xs, hs, xf, xg, zb, yb, u, part, recv, dh, dh_sent, dh_recv,
+    zf, yf, u_f, part_f, recv_f, back, sent, sent_f, load_sem, ag_send, ag_recv, rs_send, rs_recv, y_send, y_recv,
     f_send, f_recv, b_send, b_recv,
 ):
     me = lax.axis_index("seq")
@@ -126,9 +134,10 @@
         pltpu.make_async_copy(hs_hbm, hs, load_sem.at[3]),
         pltpu.make_async_copy(xs_hbm.at[0], xs, load_sem.at[4]),
         pltpu.make_async_copy(last_hbm.at[me], last, load_sem.at[5]),
+        pltpu.make_async_copy(shuffle_hbm, shuffle, load_sem.at[6]),
     ]
-    for load in loads:
-        load.start()
+    for index in (6, 0, 1, 2, 3, 4, 5):
+        loads[index].start()
 
     def spread(j, carry):
         for n in range(4):
@@ -138,10 +147,11 @@
 
     lax.fori_loop(0, TIMES, spread, 0)
     mine = pl.multiple_of(me * TIMES, TIMES)
+    loads[6].wait()
+    rows = jnp.concatenate([xf[n].astype(BF16) for n in range(4)], axis=1)
+    rows = jnp.dot(rows, shuffle[0], preferred_element_type=F32).astype(BF16)
     for c in range(CH):
-        for n in range(4):
-            value = xf[n, c * TIMES : (c + 1) * TIMES, :].astype(BF16)
-            xg[c, pl.ds(mine, TIMES), n * 128 : (n + 1) * 128] = value
+        xg[c, pl.ds(mine, TIMES), :] = rows[c * TIMES : (c + 1) * TIMES, :]
 
     pl.semaphore_wait(barrier, 5)
 
@@ -169,63 +179,79 @@
             if k < 2:
                 gather_copy(q, k + 1, False).start()
 
+    def put_split(dest, a, rows, real, imag):
+        for index, value in enumerate((real, imag)):
+            high, low = split(value)
+            for place, item in ((0, high), (2, low), (4, high)):
+                lane = (place + index) * LANES
+                dest[a, rows, lane : lane + LANES] = item
+
     def stage_a(h, lo, hi):
         def body(c, carry):
             t = jnp.dot(first[...], xg[HALF * h + c], preferred_element_type=F32)
             real = t[0:64] + t[128:192]
             imag = t[64:128] + t[192:256]
-            tc, ts = twist[0], twist[1]
-            for index, value in enumerate((real * tc + imag * ts, imag * tc - real * ts)):
-                high, low = split(value)
-                rows = pl.ds(pl.multiple_of(index * HALF * ROWS + c * ROWS, ROWS), ROWS)
-                z3[rows, 0:512] = high
-                z3[rows, 512:1024] = low
-                z3[rows, 1024:1536] = high
+            rows = pl.ds(pl.multiple_of(c * ROWS, ROWS), ROWS)
+            for a in range(4):
+                lanes = slice(a * LANES, (a + 1) * LANES)
+                tc, ts = twist[0, :, lanes], twist[1, :, lanes]
+                ar, ai = real[:, lanes], imag[:, lanes]
+                put_split(zb, a, rows, ar * tc + ai * ts, ai * tc - ar * ts)
             return carry
 
         lax.fori_loop(lo, hi, body, 0)
 
-    def columns(operand, rows, lo, hi):
-        def body(n, carry):
-            lanes = pl.ds(pl.multiple_of(n * 256, 256), 256)
-            pcs[0:rows, lanes] = jnp.dot(
-                operand[0:rows, :], wide[:, lanes], preferred_element_type=F32
-            )
+    def columns(source, dest, inverse):
+        def body(a, carry):
+            weight = wide[a + 4] if inverse else wide[a]
+            dest[a] = jnp.dot(source[a], weight, preferred_element_type=F32)
             return carry
 
-        lax.fori_loop(lo, hi, body, 0)
+        lax.fori_loop(0, 4, body, 0)
+
+    def quarters(values, forward):
+        (r0, i0), (r1, i1), (r2, i2), (r3, i3) = values
+        sr, si, dr, di = r0 + r2, i0 + i2, r0 - r2, i0 - i2
+        tr, ti, er, ei = r1 + r3, i1 + i3, r1 - r3, i1 - i3
+        left = (dr + ei, di - er)
+        right = (dr - ei, di + er)
+        if not forward:
+            left, right = right, left
+        return [(sr + tr, si + ti), left, (sr - tr, si - ti), right]
 
     def products(h, lo, hi):
         def body(c, carry):
-            rr = pl.ds(pl.multiple_of(c * ROWS, ROWS), ROWS)
-            ri = pl.ds(pl.multiple_of(HALF * ROWS + c * ROWS, ROWS), ROWS)
-            gr = pcs[rr, 0:512] + pcs[ri, 512:1024]
-            gi = pcs[ri, 0:512] - pcs[rr, 512:1024]
-            hr, hi = hs[0, HALF * h + c], hs[1, HALF * h + c]
-            for rows, value in ((rr, gr * hr + gi * hi), (ri, gi * hr - gr * hi)):
-                high, low = split(value)
-                d3[rows, 0:512] = high
-                d3[rows, 512:1024] = low
-                d3[rows, 1024:1536] = high
-            xr, xi = xs[0, HALF * h + c], xs[1, HALF * h + c]
-            dh[h, c, 0] = gr * xr + gi * xi
-            dh[h, c, 1] = gi * xr - gr * xi
+            rows = pl.ds(pl.multiple_of(c * ROWS, ROWS), ROWS)
+            bins = quarters(
+                [(yb[a, rows, 0:LANES], yb[a, rows, LANES : 2 * LANES]) for a in range(4)], True
+            )
+            channel = HALF * h + c
+            inner = []
+            for e, (gr, gi) in enumerate(bins):
+                lanes = slice(e * LANES, (e + 1) * LANES)
+                hr, hi_ = hs[0, channel, :, lanes], hs[1, channel, :, lanes]
+                inner.append((gr * hr + gi * hi_, gi * hr - gr * hi_))
+                xr, xi = xs[0, channel, :, lanes], xs[1, channel, :, lanes]
+                dh[h, c, 0, :, lanes] = gr * xr + gi * xi
+                dh[h, c, 1, :, lanes] = gi * xr - gr * xi
+            for a, (real, imag) in enumerate(quarters(inner, False)):
+                put_split(zb, a, rows, real, imag)
             return carry
 
         lax.fori_loop(lo, hi, body, 0)
 
-    def untwist(count, dest, lo, hi):
+    def untwist(source, dest, lo, hi):
         def body(c, carry):
-            rr = pl.ds(pl.multiple_of(c * ROWS, ROWS), ROWS)
-            ri = pl.ds(pl.multiple_of(count * ROWS + c * ROWS, ROWS), ROWS)
-            vr = pcs[rr, 0:512] - pcs[ri, 512:1024]
-            vi = pcs[ri, 0:512] + pcs[rr, 512:1024]
-            tc, ts = twist[0], twist[1]
-            for index, value in enumerate((vr * tc - vi * ts, vi * tc + vr * ts)):
-                high, low = split(value)
-                dest[c, 64 * index : 64 * index + 64, :] = high
-                dest[c, 128 + 64 * index : 192 + 64 * index, :] = low
-                dest[c, 256 + 64 * index : 320 + 64 * index, :] = high
+            rows = pl.ds(pl.multiple_of(c * ROWS, ROWS), ROWS)
+            for a in range(4):
+                lanes = slice(a * LANES, (a + 1) * LANES)
+                vr, vi = source[a, rows, 0:LANES], source[a, rows, LANES : 2 * LANES]
+                tc, ts = twist[0, :, lanes], twist[1, :, lanes]
+                for index, value in enumerate((vr * tc - vi * ts, vi * tc + vr * ts)):
+                    high, low = split(value)
+                    dest[c, 64 * index : 64 * index + 64, lanes] = high
+                    dest[c, 128 + 64 * index : 192 + 64 * index, lanes] = low
+                    dest[c, 256 + 64 * index : 320 + 64 * index, lanes] = high
             return carry
 
         lax.fori_loop(lo, hi, body, 0)
@@ -312,19 +338,63 @@
 
     def batch_copy(h, o):
         return pltpu.make_async_remote_copy(
-            src_ref=dh.at[h, peer(o)], dst_ref=dh_recv.at[h, o - 1],
+            src_ref=dh_sent.at[h, o - 1], dst_ref=dh_recv.at[h, o - 1],
             send_sem=y_send.at[h, o - 1], recv_sem=y_recv.at[h, o - 1],
             device_id={"dp": peer(o)}, device_id_type=MESH,
         )
 
+    tiles = [(pl.ds(16 * r, 16), pl.ds(128 * n, 128)) for r in range(ROWS // 16) for n in range(4)]
+
+    def batch_send(h):
+        for o in (1, 2, 3):
+
+            def body(index, carry):
+                def put(b, code):
+                    dh_sent[h, o - 1, index, b] = code
+
+                def put_top(top):
+                    dh_sent[h, o - 1, index, 16] = top
+
+                other = peer(o)
+                encode([dh[h, other, index, rows, lanes] for rows, lanes in tiles], put, put_top)
+                return carry
+
+            lax.fori_loop(0, 2, body, 0)
+            batch_copy(h, o).start()
+
+    def batch_sum(h):
+        for o in (1, 2, 3):
+            batch_copy(h, o).wait_recv()
+
+        def body(index, carry):
+            for o in (1, 2, 3):
+                codes = [dh_recv[h, o - 1, index, b] for b in range(16)]
+                for (rows, lanes), value in zip(tiles, decode(codes, dh_recv[h, o - 1, index, 16])):
+                    dh[h, batch, index, rows, lanes] += value
+            return carry
+
+        lax.fori_loop(0, 2, body, 0)
+        values = [
+            (
+                dh[h, batch, 0, :, e * LANES : (e + 1) * LANES],
+                dh[h, batch, 1, :, e * LANES : (e + 1) * LANES],
+            )
+            for e in range(4)
+        ]
+        for a, (real, imag) in enumerate(quarters(values, False)):
+            put_split(zf, a, slice(0, ROWS), real, imag)
+
+    def filter_part(h):
+        batch_sum(h)
+        columns(zf, yf, True)
+        untwist(yf, u_f, 0, 1)
+        stage_e(u_f, part_f, h, 0, 1)
+        reduce_start(small, h, small_way[h])
+
     def half_parts(h):
         def start_pieces(q):
             reduce_start(big, q, long_way[q])
 
-        def batch_starts():
-            for o in (1, 2, 3):
-                batch_copy(h, o).start()
-
         def wait(index):
             if h == 0:
                 loads[index].wait()
@@ -332,80 +402,59 @@
         return [
             lambda: (wait(0), wait(1), stage_a(h, 0, 2)),
             lambda: stage_a(h, 2, 4),
-            lambda: (wait(2), columns(z3, 512, 0, 2)),
-            lambda: columns(z3, 512, 2, 4),
+            lambda: (wait(2), columns(zb, yb, False)),
             lambda: (wait(3), wait(4), products(h, 0, 2)),
-            lambda: (products(h, 2, 4), batch_starts()),
-            lambda: columns(d3, 512, 0, 2),
-            lambda: columns(d3, 512, 2, 4),
-            lambda: untwist(HALF, u, 0, 2),
-            lambda: untwist(HALF, u, 2, 4),
-            lambda: (wait(5), stage_e(u, part, HALF * h, 0, 2), start_pieces(2 * h)),
-            lambda: (stage_e(u, part, HALF * h, 2, 4), start_pieces(2 * h + 1)),
+            lambda: (products(h, 2, 4), batch_send(h)),
+            lambda: columns(zb, yb, True),
+            lambda: (wait(5), untwist(yb, u, 0, 2), stage_e(u, part, HALF * h, 0, 2)),
+            lambda: start_pieces(2 * h),
+            lambda: (untwist(yb, u, 2, 4), stage_e(u, part, HALF * h, 2, 4)),
+            lambda: start_pieces(2 * h + 1),
         ]
 
+    def gather(*steps):
+        for q, k in steps:
+            gather_step(q, k)
+
+    def reduce(*steps):
+        for q, k in steps:
+            reduce_step(big, q, long_way[q], k)
+
+    def reduce_f(k):
+        for h in range(2):
+            reduce_step(small, h, small_way[h], k)
+
     def weave(parts, services):
-        done = 0
         for index, part_of in enumerate(parts):
             part_of()
-            while done * len(parts) < (index + 1) * len(services):
-                services[done]()
-                done += 1
-
-    def gather_services(pieces):
-        return [functools.partial(gather_step, q, k) for k in range(4) for q in pieces]
-
-    def reduce_services(bufs, pieces, ways, first=0):
-        return [
-            functools.partial(reduce_step, bufs, q, ways[q], k)
-            for k in range(first, 4)
-            for q in pieces
-        ]
-
-    for q in (0, 1):
+            for service in services.get(index, ()):
+                service()
+
+    for q in (0, 1, 2):
         gather_start(q)
-    for k in range(3):
-        for q in (0, 1):
-            gather_step(q, k)
-    for q in (2, 3):
-        gather_start(q)
-    for q in (0, 1):
-        gather_step(q, 3)
-    weave(half_parts(0), gather_services((2, 3)))
-    weave(half_parts(1), reduce_services(big, (0, 1), long_way))
-
-    def batch_sum(h):
-        for o in (1, 2, 3):
-            batch_copy(h, o).wait_recv()
-        for index in range(2):
-            value = (dh[h, batch, index] + dh_recv[h, 0, index]) + (
-                dh_recv[h, 1, index] + dh_recv[h, 2, index]
-            )
-            high, low = split(value)
-            rows = slice(index * 128 + h * 64, index * 128 + h * 64 + 64)
-            z3[rows, 0:512] = high
-            z3[rows, 512:1024] = low
-            z3[rows, 1024:1536] = high
-
-    filter_parts = [
-        lambda: batch_sum(0),
-        lambda: batch_sum(1),
-        lambda: columns(z3, 256, 0, 4),
-        lambda: (
-            untwist(2, u_f, 0, 2),
-            stage_e(u_f, part_f, 0, 0, 2),
-            reduce_start(small, 0, small_way[0]),
-            reduce_start(small, 1, small_way[1]),
-        ),
-    ]
-    services = reduce_services(big, (2, 3), long_way)
-    weave(filter_parts, services[:4])
-    small_services = reduce_services(small, (0, 1), small_way)
-    for index in range(4):
-        services[4 + index]()
-        small_services[index]()
-    for service in small_services[4:]:
-        service()
+    gather((0, 0), (1, 0), (2, 0), (0, 1), (1, 1))
+    gather_start(3)
+    gather((0, 2), (1, 2), (2, 1), (3, 0), (0, 3), (1, 3))
+    weave(
+        half_parts(0),
+        {
+            0: [lambda: gather((2, 2))],
+            2: [lambda: gather((3, 1))],
+            5: [lambda: gather((3, 2))],
+            7: [lambda: gather((2, 3))],
+            9: [lambda: gather((3, 3))],
+        },
+    )
+    weave(half_parts(1), {3: [lambda: reduce((0, 0))], 5: [lambda: reduce((1, 0))]})
+    reduce((0, 1), (1, 1), (2, 0), (3, 0))
+    filter_part(0)
+    reduce((0, 2), (1, 2), (2, 1), (3, 1))
+    filter_part(1)
+    reduce((0, 3), (1, 3), (2, 2), (3, 2))
+    reduce_f(0)
+    reduce((2, 3), (3, 3))
+    for k in (1, 2, 3):
+        reduce_f(k)
 
     def back_copy(h, o):
         there = pl.multiple_of(peer(o) * 8, 8)
@@ -430,6 +479,11 @@
         for c, rows, lanes, value in reduce_end(big, q):
             xf[lanes.start // 128, c * TIMES + rows.start : c * TIMES + rows.start + 16, :] = value
 
+    rows = jnp.concatenate([xf[n].astype(BF16) for n in range(4)], axis=1)
+    rows = jnp.dot(rows, shuffle[1], preferred_element_type=F32)
+    for n in range(4):
+        xf[n] = rows[:, n * 128 : (n + 1) * 128]
+
     def collect(j, carry):
         for n in range(4):
             lanes = pl.ds(pl.multiple_of(j * COLS + n * 128, 128), 128)
@@ -441,8 +495,13 @@
     for h in range(2):
         for o in (1, 2, 3):
             back_copy(h, o).wait_recv()
+    high, low = split(back[...])
+    rest = (back[...] - high.astype(F32) - low.astype(F32)).astype(BF16)
+    lines = sum(
+        jnp.dot(item, shuffle[1], preferred_element_type=F32) for item in (rest, low, high)
+    )
     for n in range(4):
-        xf[n, 0:64, :] = back[:, n * 128 : (n + 1) * 128]
+        xf[n, 0:64, :] = lines[:, n * 128 : (n + 1) * 128]
         for j in range(8):
             start = j * COLS + n * 128
             fl_ref[:, start : start + 128] = xf[n, pl.ds(j, CH, stride=8), :]
@@ -465,7 +524,7 @@
 
 
 def on_device(grad_out, input_spectrum, filter_spectrum):
-    wide, first, last, twist = (jnp.asarray(t) for t in tables())
+    wide, first, last, twist, shuffle = (jnp.asarray(t) for t in tables())
     vmem = pl.BlockSpec(memory_space=pltpu.VMEM)
     anywhere = pl.BlockSpec(memory_space=pl.ANY)
     dma = pltpu.SemaphoreType.DMA
@@ -475,32 +534,35 @@
             jax.ShapeDtypeStruct((1, CH, TIMES * COLS), BF16),
             jax.ShapeDtypeStruct((CH, TIMES * COLS // BATCHES), F32),
         ),
-        in_specs=[vmem] + [anywhere] * 6,
+        in_specs=[vmem] + [anywhere] * 7,
         out_specs=(vmem, vmem),
         scratch_shapes=[
-            pltpu.VMEM((1536, 1024), BF16),
+            pltpu.VMEM((8, 768, 256), BF16),
             pltpu.VMEM((256, 256), BF16),
             pltpu.VMEM((256, 384), BF16),
             pltpu.VMEM((2, ROWS, COLS), F32),
+            pltpu.VMEM((2, COLS, COLS), BF16),
             pltpu.VMEM((2, CH, ROWS, COLS), F32),
             pltpu.VMEM((2, CH, ROWS, COLS), F32),
             pltpu.VMEM((4, CH * TIMES, 128), F32),
             pltpu.VMEM((CH, SHARDS * TIMES, COLS), BF16),
-            pltpu.VMEM((512, 1536), BF16),
-            pltpu.VMEM((512, 1536), BF16),
-            pltpu.VMEM((512, 1024), F32),
+            pltpu.VMEM((4, HALF * ROWS, 768), BF16),
+            pltpu.VMEM((4, HALF * ROWS, 256), F32),
             pltpu.VMEM((HALF, 384, COLS), BF16),
             pltpu.VMEM((SHARDS, CH, TIMES, COLS), F32),
             pltpu.VMEM((4, 7, 17, 16, 128), BF16),
             pltpu.VMEM((2, BATCHES, 2, ROWS, COLS), F32),
-            pltpu.VMEM((2, 3, 2, ROWS, COLS), F32),
-            pltpu.VMEM((2, 384, COLS), BF16),
+            pltpu.VMEM((2, 3, 2, 17, 16, 128), BF16),
+            pltpu.VMEM((2, 3, 2, 17, 16, 128), BF16),
+            pltpu.VMEM((4, ROWS, 768), BF16),
+            pltpu.VMEM((4, ROWS, 256), F32),
+            pltpu.VMEM((1, 384, COLS), BF16),
             pltpu.VMEM((SHARDS, 2, TIMES, COLS), F32),
             pltpu.VMEM((2, 7, 9, 16, 128), BF16),
             pltpu.VMEM((CH * 8, COLS), F32),
             pltpu.VMEM((4, 7, 17, 16, 128), BF16),
             pltpu.VMEM((2, 7, 9, 16, 128), BF16),
-            dma((6,)),
+            dma((7,)),
             dma((4, 7)), dma((4, 7)),
             dma((4, 7)), dma((4, 7)),
             dma((2, 3)), dma((2, 3)),
@@ -510,7 +572,7 @@
         compiler_params=pltpu.CompilerParams(
             collective_id=0, has_side_effects=True, vmem_limit_bytes=56 * 1024 * 1024
         ),
-    )(grad_out, input_spectrum, filter_spectrum, wide, first, last, twist)
+    )(grad_out, input_spectrum, filter_spectrum, wide, first, last, twist, shuffle)
 
 
 def solution(mesh):

time: 91.6 us -> 80.1 us (0.87)
  Pallas kernels: 87.6 us -> 76.1 us
    pallas_call x1, Pallas kernels: 87.6 us -> 76.1 us  [on_device(): pl.pallas_call(kernel, out_shape=(jax.ShapeDtypeStruct((1, CH, TIMES * CO...]
where the time goes in v3:
time: 80.1 us; the launch traced here: 79.9 us
  Pallas kernels  76.1 us (95%)
  local copies, waits for them, and re-layouts  3.24 us (4%)
    pallas_call x1, Pallas kernels, on_device(): pl.pallas_call(kernel, out_shape=(jax.ShapeDtypeStruct((1, CH, TIMES * CO...  76.1 us
    unnamed x2, local copies, waits for them, and re-layouts  3.24 us

profile of v3, /device:TPU:2, one launch (start us, length us, event | category | flops | bytes accessed | tf_op | source)
XLA Modules:
  0.0 79.9 jit_solution(18337745825197968574)
XLA Ops:
  0.6 76.1 %shard_map.95 = (bf16[1,8,16384]{2,1,0:T(8,128)(2,1)}, f32[8,4096]{1,0:T(8,128)}) custom-call(bf16[1,8,16384]{2,1,0:T(8,128)(2,1)} %x_ref.1, f32[1,2,8,64,512]{4,3,2,1,0:T(8,128)} %xs_hbm.1, f32[2,8,64,512]{3,2,1,0:T(8,128)} %hs_hbm.1, bf16[8,768,256]{2,1,0:T(8,128)(2,1)} %constant.10.clone.wide_hbm, bf16[8,256,256]{2,1,0:T(8,128)(2,1)} %constant.11.clone.first_hbm, ...), custom_call_target="tpu_custom_call" | custom-call | tf_op jit(solution)/shard_map/pallas_call | solution.py:531
  76.7 1.7 %copy.12 = bf16[1,8,16384]{2,1,0:T(8,128)(2,1)} copy(bf16[1,8,16384]{2,1,0:T(8,128)(2,1)} %get-tuple-element.4) | data formatting | bytes 524288
  78.4 1.6 %copy.13 = f32[8,4096]{1,0:T(8,128)} copy(f32[8,4096]{1,0:T(8,128)} %get-tuple-element.5) | data formatting | bytes 262144

commit v4 on v3

--- a/solution.py
+++ b/solution.py
@@ -22,6 +22,37 @@
 TIMES = 32
 MODULUS = BINS * COLS
 LANES = 128
+NEAR = (1, -1, 2, -2, 3, -3)
+LONG_WAY = (1, 1, -1, -1, -1, 1, 1, -1)
+ORDER = (
+    ("gs", 0), ("gs", 1), ("gs", 2), ("gs", 3), ("gl", 0, 0), ("gr", 0, 0), ("gl", 1, 0),
+    ("gr", 1, 0), ("gl", 2, 0), ("gr", 2, 0), ("gl", 3, 0), ("gr", 3, 0), ("gl", 0, 1),
+    ("gr", 0, 1), ("gl", 1, 1), ("gr", 1, 1), ("gl", 2, 1), ("gr", 2, 1), ("gl", 3, 1), ("gs", 4),
+    ("gs", 5), ("gr", 3, 1), ("gl", 0, 2), ("gr", 0, 2), ("gl", 1, 2), ("gs", 6), ("gr", 1, 2),
+    ("gl", 2, 2), ("gr", 2, 2), ("gl", 3, 2), ("gr", 4, 0), ("gl", 4, 0), ("gl", 5, 0), ("gs", 7),
+    ("gr", 5, 0), ("gr", 3, 2), ("gr", 6, 0), ("gl", 0, 3), ("A", 0), ("gl", 2, 3), ("gl", 1, 3),
+    ("A", 1), ("A", 2), ("gl", 3, 3), ("gl", 6, 0), ("A", 3), ("B", 0), ("gl", 4, 1), ("gr", 4, 1),
+    ("gl", 7, 0), ("gl", 5, 1), ("C", 0), ("gr", 5, 1), ("gr", 7, 0), ("Y", 0), ("D", 0),
+    ("gl", 6, 1), ("gr", 6, 1), ("UE", 0), ("Rl", 0, -1), ("Rr", 0, -1), ("gl", 4, 2),
+    ("gr", 4, 2), ("UE", 1), ("Rl", 1, -1), ("Rr", 1, -1), ("gl", 5, 2), ("gl", 7, 1), ("UE", 2),
+    ("Rl", 2, -1), ("Rr", 2, -1), ("gr", 5, 2), ("gr", 7, 1), ("UE", 3), ("Rl", 3, -1),
+    ("Rr", 3, -1), ("gl", 6, 2), ("gr", 6, 2), ("Rl", 0, 0), ("Rr", 0, 0), ("Rl", 1, 0),
+    ("gl", 4, 3), ("A", 4), ("gl", 5, 3), ("Rr", 1, 0), ("A", 5), ("gl", 7, 2), ("Rr", 2, 0),
+    ("gr", 7, 2), ("Rl", 2, 0), ("Rr", 3, 0), ("Rl", 3, 0), ("F", 0), ("Fs", 0), ("Rr", 1, 1),
+    ("gl", 6, 3), ("Rl", 0, 1), ("Rr", 0, 1), ("Rl", 1, 1), ("gl", 7, 3), ("A", 6), ("A", 7),
+    ("B", 1), ("C", 1), ("Rl", 3, 1), ("Rr", 3, 1), ("Y", 1), ("Fa", 0), ("Fc", 0), ("D", 1),
+    ("Fb", 0), ("UE", 4), ("Rl", 4, -1), ("Rr", 4, -1), ("Rl", 0, 2), ("UE", 5), ("Rl", 5, -1),
+    ("Rr", 5, -1), ("Rl", 1, 2), ("UE", 6), ("Rl", 6, -1), ("Rr", 6, -1), ("Rl", 3, 2), ("UE", 7),
+    ("Rl", 7, -1), ("Rr", 7, -1), ("Rl", 2, 1), ("Rr", 2, 1), ("Rr", 1, 2), ("Rr", 0, 2),
+    ("Rr", 3, 2), ("Rr", 4, 0), ("Fend", 0), ("Rl", 0, 3), ("X", 0), ("Rl", 4, 0), ("Rl", 5, 0),
+    ("Rr", 5, 0), ("Rl", 1, 3), ("X", 1), ("Rl", 6, 0), ("F", 1), ("Fs", 1), ("Rl", 7, 0),
+    ("Rr", 7, 0), ("Rr", 6, 0), ("Rl", 3, 3), ("Rr", 2, 2), ("Rr", 4, 1), ("Rl", 2, 2), ("X", 3),
+    ("Rl", 4, 1), ("Rl", 5, 1), ("Rl", 6, 1), ("Rr", 5, 1), ("Fa", 1), ("Fc", 1), ("Fb", 1),
+    ("Rl", 7, 1), ("Rr", 7, 1), ("Rr", 6, 1), ("Rr", 4, 2), ("Rl", 5, 2), ("Rl", 2, 3), ("X", 2),
+    ("Rl", 6, 2), ("Rl", 4, 2), ("Rr", 5, 2), ("Rl", 7, 2), ("Fend", 1), ("Rr", 7, 2),
+    ("Rr", 6, 2), ("Rl", 4, 3), ("Rl", 5, 3), ("X", 4), ("X", 5), ("Rl", 6, 3), ("X", 6),
+    ("Rl", 7, 3), ("X", 7),
+)
 
 
 def split_table(table):
@@ -108,7 +139,7 @@
 def kernel(
     x_ref, xs_hbm, hs_hbm, wide_hbm, first_hbm, last_hbm, twist_hbm, shuffle_hbm,
     in_ref, fl_ref,
-    wide, first, last, twist, shuffle, xs, hs, xf, xg, zb, yb, u, part, recv, dh, dh_sent, dh_recv,
+    wide, first, last, twist, shuffle, xs, hs, xf, xg, zb, yb, db, vb, u, part, recv, dh, dh_sent, dh_recv,
     zf, yf, u_f, part_f, recv_f, back, sent, sent_f, load_sem, ag_send, ag_recv, rs_send, rs_recv, y_send, y_recv,
     f_send, f_recv, b_send, b_recv,
 ):
@@ -122,7 +153,7 @@
         return lax.rem(batch + offset, BATCHES)
 
     barrier = pltpu.get_barrier_semaphore()
-    for offset in (1, -1):
+    for offset in NEAR:
         pl.semaphore_signal(barrier, inc=1, device_id={"seq": ring(offset)}, device_id_type=MESH)
     for offset in (1, 2, 3):
         pl.semaphore_signal(barrier, inc=1, device_id={"dp": peer(offset)}, device_id_type=MESH)
@@ -153,14 +184,12 @@
     for c in range(CH):
         xg[c, pl.ds(mine, TIMES), :] = rows[c * TIMES : (c + 1) * TIMES, :]
 
-    pl.semaphore_wait(barrier, 5)
-
-    long_way = (-1, 1, -1, 1)
+    pl.semaphore_wait(barrier, len(NEAR) + 3)
 
     def gather_copy(q, k, long):
-        way = long_way[q] if long else -long_way[q]
+        way = LONG_WAY[q] if long else -LONG_WAY[q]
         source = pl.multiple_of(ring(-way * k) * TIMES, TIMES)
-        block = xg.at[pl.ds(2 * q, 2), pl.ds(source, TIMES), :]
+        block = xg.at[q, pl.ds(source, TIMES), :]
         slot = k if long else 4 + k
         return pltpu.make_async_remote_copy(
             src_ref=block, dst_ref=block, send_sem=ag_send.at[q, slot], recv_sem=ag_recv.at[q, slot],
@@ -171,13 +200,10 @@
         gather_copy(q, 0, True).start()
         gather_copy(q, 0, False).start()
 
-    def gather_step(q, k):
-        gather_copy(q, k, True).wait_recv()
-        if k < 3:
-            gather_copy(q, k + 1, True).start()
-            gather_copy(q, k, False).wait_recv()
-            if k < 2:
-                gather_copy(q, k + 1, False).start()
+    def gather_hop(q, k, long):
+        gather_copy(q, k, long).wait_recv()
+        if k < (3 if long else 2):
+            gather_copy(q, k + 1, long).start()
 
     def put_split(dest, a, rows, real, imag):
         for index, value in enumerate((real, imag)):
@@ -186,28 +212,22 @@
                 lane = (place + index) * LANES
                 dest[a, rows, lane : lane + LANES] = item
 
-    def stage_a(h, lo, hi):
-        def body(c, carry):
-            t = jnp.dot(first[...], xg[HALF * h + c], preferred_element_type=F32)
-            real = t[0:64] + t[128:192]
-            imag = t[64:128] + t[192:256]
-            rows = pl.ds(pl.multiple_of(c * ROWS, ROWS), ROWS)
-            for a in range(4):
-                lanes = slice(a * LANES, (a + 1) * LANES)
-                tc, ts = twist[0, :, lanes], twist[1, :, lanes]
-                ar, ai = real[:, lanes], imag[:, lanes]
-                put_split(zb, a, rows, ar * tc + ai * ts, ai * tc - ar * ts)
-            return carry
-
-        lax.fori_loop(lo, hi, body, 0)
+    def stage_a(q):
+        h, c = divmod(q, HALF)
+        t = jnp.dot(first[...], xg[q], preferred_element_type=F32)
+        real = t[0:64] + t[128:192]
+        imag = t[64:128] + t[192:256]
+        rows = slice(c * ROWS, (c + 1) * ROWS)
+        for a in range(4):
+            lanes = slice(a * LANES, (a + 1) * LANES)
+            tc, ts = twist[0, :, lanes], twist[1, :, lanes]
+            ar, ai = real[:, lanes], imag[:, lanes]
+            put_split(zb.at[h], a, rows, ar * tc + ai * ts, ai * tc - ar * ts)
 
     def columns(source, dest, inverse):
-        def body(a, carry):
+        for a in range(4):
             weight = wide[a + 4] if inverse else wide[a]
             dest[a] = jnp.dot(source[a], weight, preferred_element_type=F32)
-            return carry
-
-        lax.fori_loop(0, 4, body, 0)
 
     def quarters(values, forward):
         (r0, i0), (r1, i1), (r2, i2), (r3, i3) = values
@@ -219,11 +239,12 @@
             left, right = right, left
         return [(sr + tr, si + ti), left, (sr - tr, si - ti), right]
 
-    def products(h, lo, hi):
+    def products(h):
         def body(c, carry):
             rows = pl.ds(pl.multiple_of(c * ROWS, ROWS), ROWS)
             bins = quarters(
-                [(yb[a, rows, 0:LANES], yb[a, rows, LANES : 2 * LANES]) for a in range(4)], True
+                [(yb[h, a, rows, 0:LANES], yb[h, a, rows, LANES : 2 * LANES]) for a in range(4)],
+                True,
             )
             channel = HALF * h + c
             inner = []
@@ -235,106 +256,108 @@
                 dh[h, c, 0, :, lanes] = gr * xr + gi * xi
                 dh[h, c, 1, :, lanes] = gi * xr - gr * xi
             for a, (real, imag) in enumerate(quarters(inner, False)):
-                put_split(zb, a, rows, real, imag)
+                put_split(db.at[h], a, rows, real, imag)
             return carry
 
-        lax.fori_loop(lo, hi, body, 0)
-
-    def untwist(source, dest, lo, hi):
-        def body(c, carry):
-            rows = pl.ds(pl.multiple_of(c * ROWS, ROWS), ROWS)
-            for a in range(4):
-                lanes = slice(a * LANES, (a + 1) * LANES)
-                vr, vi = source[a, rows, 0:LANES], source[a, rows, LANES : 2 * LANES]
-                tc, ts = twist[0, :, lanes], twist[1, :, lanes]
-                for index, value in enumerate((vr * tc - vi * ts, vi * tc + vr * ts)):
-                    high, low = split(value)
-                    dest[c, 64 * index : 64 * index + 64, lanes] = high
-                    dest[c, 128 + 64 * index : 192 + 64 * index, lanes] = low
-                    dest[c, 256 + 64 * index : 320 + 64 * index, lanes] = high
-            return carry
-
-        lax.fori_loop(lo, hi, body, 0)
-
-    def stage_e(source, dest, base, lo, hi):
-        def body(c, carry):
-            y = jnp.dot(last[...], source[c], preferred_element_type=F32)
-            dest[:, base + c] = y.reshape(SHARDS, TIMES, COLS)
-            return carry
-
-        lax.fori_loop(lo, hi, body, 0)
-
-    def reduce_copy(bufs, q, way, k, long):
-        _, sent_ref, recv_ref, send, received, _ = bufs
+        lax.fori_loop(0, HALF, body, 0)
+
+    def finish(source, c, buffer, dest, channel):
+        rows = slice(c * ROWS, (c + 1) * ROWS)
+        for a in range(4):
+            lanes = slice(a * LANES, (a + 1) * LANES)
+            vr, vi = source[a, rows, 0:LANES], source[a, rows, LANES : 2 * LANES]
+            tc, ts = twist[0, :, lanes], twist[1, :, lanes]
+            for index, value in enumerate((vr * tc - vi * ts, vi * tc + vr * ts)):
+                high, low = split(value)
+                buffer[64 * index : 64 * index + 64, lanes] = high
+                buffer[128 + 64 * index : 192 + 64 * index, lanes] = low
+                buffer[256 + 64 * index : 320 + 64 * index, lanes] = high
+        y = jnp.dot(last[...], buffer[...], preferred_element_type=F32)
+        dest[:, channel] = y.reshape(SHARDS, TIMES, COLS)
+
+    def share(part_ref, dest, c):
+        return [part_ref[dest, c, rows, lanes] for rows, lanes in lines_of]
+
+    lines_of = [
+        (pl.ds(16 * r, 16), pl.ds(128 * n, 128)) for r in range(TIMES // 16) for n in range(4)
+    ]
+
+    def read(ref, q, slot):
+        return decode([ref[q, slot, b] for b in range(8)], ref[q, slot, 8])
+
+    def write(ref, q, slot, values):
+        def put(index, code):
+            ref[q, slot, index] = code
+
+        def put_top(top):
+            ref[q, slot, 8] = top
+
+        encode(values, put, put_top)
+
+    def add(left, right):
+        return [a + b for a, b in zip(left, right)]
+
+    def reduce_copy(q, k, long):
         slot = k if long else 4 + k
+        way = LONG_WAY[q] if long else -LONG_WAY[q]
         return pltpu.make_async_remote_copy(
-            src_ref=sent_ref.at[q, slot], dst_ref=recv_ref.at[q, slot],
-            send_sem=send.at[q, slot], recv_sem=received.at[q, slot],
-            device_id={"seq": ring(way if long else -way)}, device_id_type=MESH,
+            src_ref=sent.at[q, slot], dst_ref=recv.at[q, slot],
+            send_sem=rs_send.at[q, slot], recv_sem=rs_recv.at[q, slot],
+            device_id={"seq": ring(way)}, device_id_type=MESH,
         )
 
-    def blocks(bufs, q):
-        n_c = bufs[5]
-        return [
-            (n_c * q + c, pl.ds(16 * r, 16), pl.ds(128 * n, 128))
-            for c in range(n_c)
-            for r in range(TIMES // 16)
-            for n in range(COLS // 128)
-        ]
-
-    def arrived(bufs, q, slot):
-        recv_ref = bufs[2]
-        count = len(blocks(bufs, q))
-        return decode([recv_ref[q, slot, b] for b in range(count)], recv_ref[q, slot, count])
-
-    def reduce_send(bufs, q, way, k, long, values):
-        sent_ref = bufs[1]
-        slot = k if long else 4 + k
-
-        def put(index, code):
-            sent_ref[q, slot, index] = code
-
-        def put_top(top):
-            sent_ref[q, slot, len(values)] = top
-
-        encode(values, put, put_top)
-        reduce_copy(bufs, q, way, k, long).start()
-
-    def reduce_hop(bufs, q, way, k, long):
-        part_ref = bufs[0]
+    def reduce_hop(q, k, long):
         hops = 4 if long else 3
-        slot = k if long else 4 + k
-        dest = ring((way if long else -way) * (hops - 1 - k))
+        way = LONG_WAY[q] if long else -LONG_WAY[q]
+        base = 0 if long else 4
         if k >= 0:
-            reduce_copy(bufs, q, way, k, long).wait_recv()
+            reduce_copy(q, k, long).wait_recv()
         if k == hops - 1:
             return
-        values = [part_ref[dest, c, rows, lanes] for c, rows, lanes in blocks(bufs, q)]
+        values = share(part, ring(way * (hops - 1 - k)), q)
         if k >= 0:
-            values = [a + b for a, b in zip(values, arrived(bufs, q, slot))]
-        reduce_send(bufs, q, way, k + 1, long, values)
-
-    def reduce_start(bufs, q, way):
-        reduce_hop(bufs, q, way, -1, True)
-        reduce_hop(bufs, q, way, -1, False)
-
-    def reduce_step(bufs, q, way, k):
-        reduce_hop(bufs, q, way, k, True)
-        if k < 3:
-            reduce_hop(bufs, q, way, k, False)
-
-    def reduce_end(bufs, q):
-        part_ref = bufs[0]
-        return [
-            (c, rows, lanes, part_ref[me, c, rows, lanes] + (a + b))
-            for (c, rows, lanes), a, b in zip(
-                blocks(bufs, q), arrived(bufs, q, 3), arrived(bufs, q, 6)
-            )
+            values = add(values, read(recv, q, base + k))
+        write(sent, q, base + k + 1, values)
+        reduce_copy(q, k + 1, long).start()
+
+    def reduce_end(q):
+        values = add(share(part, me, q), add(read(recv, q, 3), read(recv, q, 6)))
+        for (rows, lanes), value in zip(lines_of, values):
+            xf[lanes.start // 128, q * TIMES + rows.start : q * TIMES + rows.start + 16, :] = value
+
+    def pair_copy(h, slot):
+        way = 1 if h else -1
+        return pltpu.make_async_remote_copy(
+            src_ref=sent_f.at[h, slot], dst_ref=recv_f.at[h, slot],
+            send_sem=f_send.at[h, slot], recv_sem=f_recv.at[h, slot],
+            device_id={"seq": ring(way * (1, 1, -1, -1, 3, 1, -2)[slot])}, device_id_type=MESH,
+        )
+
+    def pair_send(h, slot, offset, arrived=None):
+        values = share(part_f, ring(offset * (1 if h else -1)), h)
+        if arrived is not None:
+            pair_copy(h, arrived).wait_recv()
+            values = add(values, read(recv_f, h, arrived))
+        write(sent_f, h, slot, values)
+        pair_copy(h, slot).start()
+
+    def pair_start(h):
+        for slot, offset in ((0, 4), (1, 2), (2, -3), (3, -1)):
+            pair_send(h, slot, offset)
+
+    def pair_end(h):
+        values = share(part_f, me, h)
+        for slot in (3, 4, 5, 6):
+            pair_copy(h, slot).wait_recv()
+            values = add(values, read(recv_f, h, slot))
+        for (rows, lanes), value in zip(lines_of, values):
+            part_f[me, h, rows, lanes] = value
+        for o in (1, 2, 3):
+            back_copy(h, o).start()
+        here = pl.multiple_of(batch * 8, 8)
+        back[pl.ds(pl.multiple_of((HALF * h + batch) * 8, 8), 8), :] = part_f[
+            me, h, pl.ds(here, 8), :
         ]
-
-    big = (part, sent, recv, rs_send, rs_recv, 2)
-    small = (part_f, sent_f, recv_f, f_send, f_recv, 1)
-    small_way = (-1, 1)
 
     def batch_copy(h, o):
         return pltpu.make_async_remote_copy(
@@ -387,74 +410,7 @@
     def filter_part(h):
         batch_sum(h)
         columns(zf, yf, True)
-        untwist(yf, u_f, 0, 1)
-        stage_e(u_f, part_f, h, 0, 1)
-        reduce_start(small, h, small_way[h])
-
-    def half_parts(h):
-        def start_pieces(q):
-            reduce_start(big, q, long_way[q])
-
-        def wait(index):
-            if h == 0:
-                loads[index].wait()
-
-        return [
-            lambda: (wait(0), wait(1), stage_a(h, 0, 2)),
-            lambda: stage_a(h, 2, 4),
-            lambda: (wait(2), columns(zb, yb, False)),
-            lambda: (wait(3), wait(4), products(h, 0, 2)),
-            lambda: (products(h, 2, 4), batch_send(h)),
-            lambda: columns(zb, yb, True),
-            lambda: (wait(5), untwist(yb, u, 0, 2), stage_e(u, part, HALF * h, 0, 2)),
-            lambda: start_pieces(2 * h),
-            lambda: (untwist(yb, u, 2, 4), stage_e(u, part, HALF * h, 2, 4)),
-            lambda: start_pieces(2 * h + 1),
-        ]
-
-    def gather(*steps):
-        for q, k in steps:
-            gather_step(q, k)
-
-    def reduce(*steps):
-        for q, k in steps:
-            reduce_step(big, q, long_way[q], k)
-
-    def reduce_f(k):
-        for h in range(2):
-            reduce_step(small, h, small_way[h], k)
-
-    def weave(parts, services):
-        for index, part_of in enumerate(parts):
-            part_of()
-            for service in services.get(index, ()):
-                service()
-
-    for q in (0, 1, 2):
-        gather_start(q)
-    gather((0, 0), (1, 0), (2, 0), (0, 1), (1, 1))
-    gather_start(3)
-    gather((0, 2), (1, 2), (2, 1), (3, 0), (0, 3), (1, 3))
-    weave(
-        half_parts(0),
-        {
-            0: [lambda: gather((2, 2))],
-            2: [lambda: gather((3, 1))],
-            5: [lambda: gather((3, 2))],
-            7: [lambda: gather((2, 3))],
-            9: [lambda: gather((3, 3))],
-        },
-    )
-    weave(half_parts(1), {3: [lambda: reduce((0, 0))], 5: [lambda: reduce((1, 0))]})
-    reduce((0, 1), (1, 1), (2, 0), (3, 0))
-    filter_part(0)
-    reduce((0, 2), (1, 2), (2, 1), (3, 1))
-    filter_part(1)
-    reduce((0, 3), (1, 3), (2, 2), (3, 2))
-    reduce_f(0)
-    reduce((2, 3), (3, 3))
-    for k in (1, 2, 3):
-        reduce_f(k)
+        finish(yf, 0, u_f, part_f, h)
 
     def back_copy(h, o):
         there = pl.multiple_of(peer(o) * 8, 8)
@@ -465,19 +421,54 @@
             device_id={"dp": peer(o)}, device_id_type=MESH,
         )
 
-    for h in range(2):
-        for c, rows, lanes, value in reduce_end(small, h):
-            part_f[me, c, rows, lanes] = value
-        for o in (1, 2, 3):
-            back_copy(h, o).start()
-        here = pl.multiple_of(batch * 8, 8)
-        back[pl.ds(pl.multiple_of((HALF * h + batch) * 8, 8), 8), :] = part_f[
-            me, h, pl.ds(here, 8), :
-        ]
-
-    for q in range(4):
-        for c, rows, lanes, value in reduce_end(big, q):
-            xf[lanes.start // 128, c * TIMES + rows.start : c * TIMES + rows.start + 16, :] = value
+    waited = set()
+
+    def need(*indices):
+        for index in indices:
+            if index not in waited:
+                waited.add(index)
+                loads[index].wait()
+
+    def run(kind, q, k=None):
+        if kind == "gs":
+            gather_start(q)
+        elif kind in ("gl", "gr"):
+            gather_hop(q, k, kind == "gl")
+        elif kind == "A":
+            need(0, 1)
+            stage_a(q)
+        elif kind == "B":
+            need(2)
+            columns(zb.at[q], yb.at[q], False)
+        elif kind == "C":
+            need(3, 4)
+            products(q)
+        elif kind == "Y":
+            batch_send(q)
+        elif kind == "D":
+            columns(db.at[q], vb.at[q], True)
+        elif kind == "UE":
+            need(5)
+            finish(vb.at[q // HALF], q % HALF, u.at[q % HALF], part, q)
+        elif kind in ("Rl", "Rr"):
+            reduce_hop(q, k, kind == "Rl")
+        elif kind == "X":
+            reduce_end(q)
+        elif kind == "F":
+            filter_part(q)
+        elif kind == "Fs":
+            pair_start(q)
+        elif kind == "Fa":
+            pair_send(q, 4, 3, 0)
+        elif kind == "Fb":
+            pair_send(q, 5, 1, 1)
+        elif kind == "Fc":
+            pair_send(q, 6, -2, 2)
+        elif kind == "Fend":
+            pair_end(q)
+
+    for task in ORDER:
+        run(*task)
 
     rows = jnp.concatenate([xf[n].astype(BF16) for n in range(4)], axis=1)
     rows = jnp.dot(rows, shuffle[1], preferred_element_type=F32)
@@ -506,21 +497,19 @@
             start = j * COLS + n * 128
             fl_ref[:, start : start + 128] = xf[n, pl.ds(j, CH, stride=8), :]
 
-    for q in range(4):
+    for q in range(CH):
         for k in range(4):
             gather_copy(q, k, True).wait_send()
-            reduce_copy(big, q, long_way[q], k, True).wait_send()
+            reduce_copy(q, k, True).wait_send()
             if k < 3:
                 gather_copy(q, k, False).wait_send()
-                reduce_copy(big, q, long_way[q], k, False).wait_send()
-    for q in range(2):
-        for k in range(4):
-            reduce_copy(small, q, small_way[q], k, True).wait_send()
-            if k < 3:
-                reduce_copy(small, q, small_way[q], k, False).wait_send()
+                reduce_copy(q, k, False).wait_send()
+    for h in range(2):
+        for slot in range(7):
+            pair_copy(h, slot).wait_send()
         for o in (1, 2, 3):
-            batch_copy(q, o).wait_send()
-            back_copy(q, o).wait_send()
+            batch_copy(h, o).wait_send()
+            back_copy(h, o).wait_send()
 
 
 def on_device(grad_out, input_spectrum, filter_spectrum):
@@ -546,25 +535,27 @@
             pltpu.VMEM((2, CH, ROWS, COLS), F32),
             pltpu.VMEM((4, CH * TIMES, 128), F32),
             pltpu.VMEM((CH, SHARDS * TIMES, COLS), BF16),
-            pltpu.VMEM((4, HALF * ROWS, 768), BF16),
-            pltpu.VMEM((4, HALF * ROWS, 256), F32),
+            pltpu.VMEM((2, 4, HALF * ROWS, 768), BF16),
+            pltpu.VMEM((2, 4, HALF * ROWS, 256), F32),
+            pltpu.VMEM((2, 4, HALF * ROWS, 768), BF16),
+            pltpu.VMEM((2, 4, HALF * ROWS, 256), F32),
             pltpu.VMEM((HALF, 384, COLS), BF16),
             pltpu.VMEM((SHARDS, CH, TIMES, COLS), F32),
-            pltpu.VMEM((4, 7, 17, 16, 128), BF16),
+            pltpu.VMEM((CH, 7, 9, 16, 128), BF16),
             pltpu.VMEM((2, BATCHES, 2, ROWS, COLS), F32),
             pltpu.VMEM((2, 3, 2, 17, 16, 128), BF16),
             pltpu.VMEM((2, 3, 2, 17, 16, 128), BF16),
             pltpu.VMEM((4, ROWS, 768), BF16),
             pltpu.VMEM((4, ROWS, 256), F32),
-            pltpu.VMEM((1, 384, COLS), BF16),
+            pltpu.VMEM((384, COLS), BF16),
             pltpu.VMEM((SHARDS, 2, TIMES, COLS), F32),
             pltpu.VMEM((2, 7, 9, 16, 128), BF16),
             pltpu.VMEM((CH * 8, COLS), F32),
-            pltpu.VMEM((4, 7, 17, 16, 128), BF16),
+            pltpu.VMEM((CH, 7, 9, 16, 128), BF16),
             pltpu.VMEM((2, 7, 9, 16, 128), BF16),
             dma((7,)),
-            dma((4, 7)), dma((4, 7)),
-            dma((4, 7)), dma((4, 7)),
+            dma((CH, 7)), dma((CH, 7)),
+            dma((CH, 7)), dma((CH, 7)),
             dma((2, 3)), dma((2, 3)),
             dma((2, 7)), dma((2, 7)),
             dma((2, 3)), dma((2, 3)),

time: 80.1 us -> 72.8 us (0.909)
  Pallas kernels: 76.1 us -> 68.6 us
    pallas_call x1, Pallas kernels: 76.1 us -> 68.6 us  [on_device(): pl.pallas_call(kernel, out_shape=(jax.ShapeDtypeStruct((1, CH, TIMES * CO...]
where the time goes in v4:
time: 72.8 us; the launch traced here: 72.5 us
  Pallas kernels  68.6 us (94%)
  local copies, waits for them, and re-layouts  3.24 us (4%)
    pallas_call x1, Pallas kernels, on_device(): pl.pallas_call(kernel, out_shape=(jax.ShapeDtypeStruct((1, CH, TIMES * CO...  68.6 us
    unnamed x2, local copies, waits for them, and re-layouts  3.24 us

profile of v4, /device:TPU:2, one launch (start us, length us, event | category | flops | bytes accessed | tf_op | source)
XLA Modules:
  0.0 72.5 jit_solution(11618919505657520562)
XLA Ops:
  0.6 68.6 %shard_map.95 = (bf16[1,8,16384]{2,1,0:T(8,128)(2,1)}, f32[8,4096]{1,0:T(8,128)}) custom-call(bf16[1,8,16384]{2,1,0:T(8,128)(2,1)} %x_ref.1, f32[1,2,8,64,512]{4,3,2,1,0:T(8,128)} %xs_hbm.1, f32[2,8,64,512]{3,2,1,0:T(8,128)} %hs_hbm.1, bf16[8,768,256]{2,1,0:T(8,128)(2,1)} %constant.10.clone.wide_hbm, bf16[8,256,256]{2,1,0:T(8,128)(2,1)} %constant.11.clone.first_hbm, ...), custom_call_target="tpu_custom_call" | custom-call | tf_op jit(solution)/shard_map/pallas_call | solution.py:520
  69.3 1.7 %copy.12 = bf16[1,8,16384]{2,1,0:T(8,128)(2,1)} copy(bf16[1,8,16384]{2,1,0:T(8,128)(2,1)} %get-tuple-element.4) | data formatting | bytes 524288
  70.9 1.6 %copy.13 = f32[8,4096]{1,0:T(8,128)} copy(f32[8,4096]{1,0:T(8,128)} %get-tuple-element.5) | data formatting | bytes 262144

commit v5 on v4

--- a/solution.py
+++ b/solution.py
@@ -23,35 +23,37 @@
 MODULUS = BINS * COLS
 LANES = 128
 NEAR = (1, -1, 2, -2, 3, -3)
-LONG_WAY = (1, 1, -1, -1, -1, 1, 1, -1)
+CHAIN_WAY = -1
+LONG_WAY = (1, 1, 1, 1, -1, -1, -1, -1)
 ORDER = (
     ("gs", 0), ("gs", 1), ("gs", 2), ("gs", 3), ("gl", 0, 0), ("gr", 0, 0), ("gl", 1, 0),
     ("gr", 1, 0), ("gl", 2, 0), ("gr", 2, 0), ("gl", 3, 0), ("gr", 3, 0), ("gl", 0, 1),
-    ("gr", 0, 1), ("gl", 1, 1), ("gr", 1, 1), ("gl", 2, 1), ("gr", 2, 1), ("gl", 3, 1), ("gs", 4),
-    ("gs", 5), ("gr", 3, 1), ("gl", 0, 2), ("gr", 0, 2), ("gl", 1, 2), ("gs", 6), ("gr", 1, 2),
-    ("gl", 2, 2), ("gr", 2, 2), ("gl", 3, 2), ("gr", 4, 0), ("gl", 4, 0), ("gl", 5, 0), ("gs", 7),
-    ("gr", 5, 0), ("gr", 3, 2), ("gr", 6, 0), ("gl", 0, 3), ("A", 0), ("gl", 2, 3), ("gl", 1, 3),
-    ("A", 1), ("A", 2), ("gl", 3, 3), ("gl", 6, 0), ("A", 3), ("B", 0), ("gl", 4, 1), ("gr", 4, 1),
-    ("gl", 7, 0), ("gl", 5, 1), ("C", 0), ("gr", 5, 1), ("gr", 7, 0), ("Y", 0), ("D", 0),
-    ("gl", 6, 1), ("gr", 6, 1), ("UE", 0), ("Rl", 0, -1), ("Rr", 0, -1), ("gl", 4, 2),
-    ("gr", 4, 2), ("UE", 1), ("Rl", 1, -1), ("Rr", 1, -1), ("gl", 5, 2), ("gl", 7, 1), ("UE", 2),
-    ("Rl", 2, -1), ("Rr", 2, -1), ("gr", 5, 2), ("gr", 7, 1), ("UE", 3), ("Rl", 3, -1),
-    ("Rr", 3, -1), ("gl", 6, 2), ("gr", 6, 2), ("Rl", 0, 0), ("Rr", 0, 0), ("Rl", 1, 0),
-    ("gl", 4, 3), ("A", 4), ("gl", 5, 3), ("Rr", 1, 0), ("A", 5), ("gl", 7, 2), ("Rr", 2, 0),
-    ("gr", 7, 2), ("Rl", 2, 0), ("Rr", 3, 0), ("Rl", 3, 0), ("F", 0), ("Fs", 0), ("Rr", 1, 1),
-    ("gl", 6, 3), ("Rl", 0, 1), ("Rr", 0, 1), ("Rl", 1, 1), ("gl", 7, 3), ("A", 6), ("A", 7),
-    ("B", 1), ("C", 1), ("Rl", 3, 1), ("Rr", 3, 1), ("Y", 1), ("Fa", 0), ("Fc", 0), ("D", 1),
-    ("Fb", 0), ("UE", 4), ("Rl", 4, -1), ("Rr", 4, -1), ("Rl", 0, 2), ("UE", 5), ("Rl", 5, -1),
-    ("Rr", 5, -1), ("Rl", 1, 2), ("UE", 6), ("Rl", 6, -1), ("Rr", 6, -1), ("Rl", 3, 2), ("UE", 7),
-    ("Rl", 7, -1), ("Rr", 7, -1), ("Rl", 2, 1), ("Rr", 2, 1), ("Rr", 1, 2), ("Rr", 0, 2),
-    ("Rr", 3, 2), ("Rr", 4, 0), ("Fend", 0), ("Rl", 0, 3), ("X", 0), ("Rl", 4, 0), ("Rl", 5, 0),
-    ("Rr", 5, 0), ("Rl", 1, 3), ("X", 1), ("Rl", 6, 0), ("F", 1), ("Fs", 1), ("Rl", 7, 0),
-    ("Rr", 7, 0), ("Rr", 6, 0), ("Rl", 3, 3), ("Rr", 2, 2), ("Rr", 4, 1), ("Rl", 2, 2), ("X", 3),
-    ("Rl", 4, 1), ("Rl", 5, 1), ("Rl", 6, 1), ("Rr", 5, 1), ("Fa", 1), ("Fc", 1), ("Fb", 1),
-    ("Rl", 7, 1), ("Rr", 7, 1), ("Rr", 6, 1), ("Rr", 4, 2), ("Rl", 5, 2), ("Rl", 2, 3), ("X", 2),
-    ("Rl", 6, 2), ("Rl", 4, 2), ("Rr", 5, 2), ("Rl", 7, 2), ("Fend", 1), ("Rr", 7, 2),
-    ("Rr", 6, 2), ("Rl", 4, 3), ("Rl", 5, 3), ("X", 4), ("X", 5), ("Rl", 6, 3), ("X", 6),
-    ("Rl", 7, 3), ("X", 7),
+    ("gr", 0, 1), ("gl", 1, 1), ("gr", 1, 1), ("gl", 2, 1), ("gr", 2, 1), ("gl", 3, 1), ("gs", 5),
+    ("gr", 3, 1), ("gl", 0, 2), ("gr", 0, 2), ("gl", 1, 2), ("gr", 1, 2), ("gs", 4), ("gs", 7),
+    ("gl", 2, 2), ("gr", 2, 2), ("gl", 3, 2), ("gs", 6), ("gl", 5, 0), ("gr", 5, 0), ("gr", 3, 2),
+    ("gl", 0, 3), ("A", 0), ("gl", 4, 0), ("gl", 1, 3), ("A", 1), ("gl", 7, 0), ("gr", 4, 0),
+    ("gl", 6, 0), ("gr", 7, 0), ("gl", 5, 1), ("gl", 2, 3), ("A", 2), ("gl", 4, 1), ("gl", 3, 3),
+    ("A", 3), ("B", 0), ("gl", 6, 1), ("gr", 6, 0), ("gl", 7, 1), ("gr", 5, 1), ("C", 0),
+    ("gl", 5, 2), ("gr", 4, 1), ("Y", 0), ("gl", 4, 2), ("D", 0), ("gr", 7, 1), ("UE", 0),
+    ("gl", 6, 2), ("gr", 6, 1), ("Rl", 0, -1), ("Rr", 0, -1), ("UE", 1), ("gl", 7, 2),
+    ("gr", 5, 2), ("Rl", 1, -1), ("Rr", 1, -1), ("UE", 2), ("gl", 5, 3), ("Rl", 2, -1),
+    ("Rr", 2, -1), ("gr", 4, 2), ("A", 5), ("gl", 4, 3), ("A", 4), ("gr", 7, 2), ("UE", 3),
+    ("gl", 6, 3), ("gr", 6, 2), ("Rl", 3, -1), ("Rr", 3, -1), ("A", 6), ("Rr", 0, 0), ("Rl", 0, 0),
+    ("gl", 7, 3), ("A", 7), ("Rl", 1, 0), ("B", 1), ("Rr", 1, 0), ("Rl", 2, 0), ("C", 1),
+    ("Rl", 3, 0), ("Rr", 2, 0), ("Rr", 3, 0), ("Y", 1), ("Rl", 0, 1), ("F", 0), ("Rr", 0, 1),
+    ("Rl", 1, 1), ("Rr", 1, 1), ("Rl", 2, 1), ("Fs", 0), ("D", 1), ("Rl", 3, 1), ("Rr", 2, 1),
+    ("Rl", 0, 2), ("Rr", 3, 1), ("UE", 4), ("Rl", 4, -1), ("Rr", 4, -1), ("UE", 5), ("Rl", 1, 2),
+    ("Rl", 5, -1), ("Rr", 5, -1), ("Rr", 0, 2), ("UE", 6), ("Rl", 2, 2), ("Rl", 6, -1),
+    ("Rr", 6, -1), ("UE", 7), ("Fl", 0, 0), ("Fr", 0, 0), ("Rl", 7, -1), ("Rr", 7, -1),
+    ("Rr", 1, 2), ("Rl", 3, 2), ("Rr", 2, 2), ("Rr", 3, 2), ("Rl", 0, 3), ("X", 0), ("Rl", 4, 0),
+    ("F", 1), ("Fs", 1), ("Rl", 6, 0), ("Rr", 4, 0), ("Rl", 5, 0), ("Rr", 5, 0), ("Rl", 1, 3),
+    ("Fl", 0, 1), ("Rl", 2, 3), ("X", 1), ("X", 2), ("Rl", 7, 0), ("Rr", 6, 0), ("Rl", 4, 1),
+    ("Fr", 0, 1), ("Fc", 1), ("Rr", 7, 0), ("Rl", 3, 3), ("X", 3), ("Rl", 6, 1), ("Fa", 1),
+    ("Rl", 5, 1), ("Fb", 1), ("Fl", 0, 2), ("Rr", 4, 1), ("Rl", 7, 1), ("Rr", 5, 1), ("Rl", 4, 2),
+    ("Rr", 6, 1), ("Fr", 0, 2), ("Rr", 7, 1), ("Rl", 6, 2), ("Rl", 5, 2), ("Fl", 0, 3),
+    ("Fend", 0), ("Rl", 7, 2), ("Fend", 1), ("Rl", 4, 3), ("Rr", 4, 2), ("X", 4), ("Rl", 6, 3),
+    ("Rr", 5, 2), ("Rl", 5, 3), ("Rr", 6, 2), ("X", 5), ("X", 6), ("Rl", 7, 3), ("Rr", 7, 2),
+    ("X", 7),
 )
 
 
@@ -341,14 +343,37 @@
         write(sent_f, h, slot, values)
         pair_copy(h, slot).start()
 
+    def chain_copy(h, k, long):
+        slot = k if long else 4 + k
+        return pltpu.make_async_remote_copy(
+            src_ref=sent_f.at[h, slot], dst_ref=recv_f.at[h, slot],
+            send_sem=f_send.at[h, slot], recv_sem=f_recv.at[h, slot],
+            device_id={"seq": ring(CHAIN_WAY if long else -CHAIN_WAY)}, device_id_type=MESH,
+        )
+
+    def chain_hop(h, k, long):
+        hops = 4 if long else 3
+        base = 0 if long else 4
+        if k >= 0:
+            chain_copy(h, k, long).wait_recv()
+        if k == hops - 1:
+            return
+        way = CHAIN_WAY if long else -CHAIN_WAY
+        values = share(part_f, ring(way * (hops - 1 - k)), h)
+        if k >= 0:
+            values = add(values, read(recv_f, h, base + k))
+        write(sent_f, h, base + k + 1, values)
+        chain_copy(h, k + 1, long).start()
+
     def pair_start(h):
         for slot, offset in ((0, 4), (1, 2), (2, -3), (3, -1)):
             pair_send(h, slot, offset)
 
     def pair_end(h):
         values = share(part_f, me, h)
-        for slot in (3, 4, 5, 6):
-            pair_copy(h, slot).wait_recv()
+        for slot in (3, 6) if h == 0 else (3, 4, 5, 6):
+            if h:
+                pair_copy(h, slot).wait_recv()
             values = add(values, read(recv_f, h, slot))
         for (rows, lanes), value in zip(lines_of, values):
             part_f[me, h, rows, lanes] = value
@@ -456,6 +481,11 @@
             reduce_end(q)
         elif kind == "F":
             filter_part(q)
+        elif kind == "Fs" and q == 0:
+            chain_hop(q, -1, True)
+            chain_hop(q, -1, False)
+        elif kind in ("Fl", "Fr"):
+            chain_hop(q, k, kind == "Fl")
         elif kind == "Fs":
             pair_start(q)
         elif kind == "Fa":
@@ -506,10 +536,18 @@
                 reduce_copy(q, k, False).wait_send()
     for h in range(2):
         for slot in range(7):
-            pair_copy(h, slot).wait_send()
+            if h:
+                pair_copy(h, slot).wait_send()
+            else:
+                chain_copy(h, slot % 4, slot < 4).wait_send()
         for o in (1, 2, 3):
             batch_copy(h, o).wait_send()
             back_copy(h, o).wait_send()
+
+
+def hand_on(in_a, in_b, out_a, out_b):
+    out_a[...] = in_a[...]
+    out_b[...] = in_b[...]
 
 
 def on_device(grad_out, input_spectrum, filter_spectrum):
@@ -517,12 +555,13 @@
     vmem = pl.BlockSpec(memory_space=pltpu.VMEM)
     anywhere = pl.BlockSpec(memory_space=pl.ANY)
     dma = pltpu.SemaphoreType.DMA
-    return pl.pallas_call(
+    out_shape = (
+        jax.ShapeDtypeStruct((1, CH, TIMES * COLS), BF16),
+        jax.ShapeDtypeStruct((CH, TIMES * COLS // BATCHES), F32),
+    )
+    results = pl.pallas_call(
         kernel,
-        out_shape=(
-            jax.ShapeDtypeStruct((1, CH, TIMES * COLS), BF16),
-            jax.ShapeDtypeStruct((CH, TIMES * COLS // BATCHES), F32),
-        ),
+        out_shape=out_shape,
         in_specs=[vmem] + [anywhere] * 7,
         out_specs=(vmem, vmem),
         scratch_shapes=[
@@ -564,6 +603,12 @@
             collective_id=0, has_side_effects=True, vmem_limit_bytes=56 * 1024 * 1024
         ),
     )(grad_out, input_spectrum, filter_spectrum, wide, first, last, twist, shuffle)
+    return pl.pallas_call(
+        hand_on,
+        out_shape=out_shape,
+        in_specs=[vmem] * 2,
+        out_specs=(vmem,) * 2,
+    )(*results)
 
 
 def solution(mesh):

time: 72.8 us -> 70.8 us (0.973)
  local copies, waits for them, and re-layouts: 3.24 us -> 0 us
  Pallas kernels: 68.6 us -> 70 us
    unnamed x2 -> x0, local copies, waits for them, and re-layouts: 3.24 us -> none
    pallas_call x1 -> x2, Pallas kernels: 68.6 us -> 70 us  [the longest x1 68.2 us: on_device(): pl.pallas_call(kernel, out_shape=out_shape, in_specs=[vmem] + [anywhere]...]
where the time goes in v5:
time: 70.8 us; the launch traced here: 70.6 us
  Pallas kernels  70 us (99%)
    pallas_call x1, Pallas kernels, on_device(): pl.pallas_call(kernel, out_shape=out_shape, in_specs=[vmem] + [anywhere]...  68.2 us
    pallas_call x1, Pallas kernels, on_device(): pl.pallas_call(hand_on, out_shape=out_shape, in_specs=[vmem] * 2, out_spe...  1.74 us

profile of v5, /device:TPU:2, one launch (start us, length us, event | category | flops | bytes accessed | tf_op | source)
XLA Modules:
  0.0 70.6 jit_solution(16857650224909850227)
XLA Ops:
  0.6 68.2 %shard_map.95 = (bf16[1,8,16384]{2,1,0:T(8,128)(2,1)}, f32[8,4096]{1,0:T(8,128)}) custom-call(bf16[1,8,16384]{2,1,0:T(8,128)(2,1)} %x_ref.1, f32[1,2,8,64,512]{4,3,2,1,0:T(8,128)} %xs_hbm.1, f32[2,8,64,512]{3,2,1,0:T(8,128)} %hs_hbm.1, bf16[8,768,256]{2,1,0:T(8,128)(2,1)} %constant.10.clone.wide_hbm, bf16[8,256,256]{2,1,0:T(8,128)(2,1)} %constant.11.clone.first_hbm, ...), custom_call_target="tpu_custom_call" | custom-call | tf_op jit(solution)/shard_map/pallas_call | solution.py:562
  68.9 1.7 %shard_map.96 = (bf16[1,8,16384]{2,1,0:T(8,128)(2,1)}, f32[8,4096]{1,0:T(8,128)}) custom-call(bf16[1,8,16384]{2,1,0:T(8,128)(2,1)} %get-tuple-element.4.in_a, f32[8,4096]{1,0:T(8,128)} %get-tuple-element.5.in_b), custom_call_target="tpu_custom_call" | custom-call | tf_op jit(solution)/shard_map/pallas_call | solution.py:606

commit v6 on v5

--- a/solution.py
+++ b/solution.py
@@ -139,9 +139,9 @@
 
 
 def kernel(
-    x_ref, xs_hbm, hs_hbm, wide_hbm, first_hbm, last_hbm, twist_hbm, shuffle_hbm,
+    x_hbm, xs_hbm, hs_hbm, wide_hbm, first_hbm, last_hbm, twist_hbm, shuffle_hbm,
     in_ref, fl_ref,
-    wide, first, last, twist, shuffle, xs, hs, xf, xg, zb, yb, db, vb, u, part, recv, dh, dh_sent, dh_recv,
+    x_ref, wide, first, last, twist, shuffle, xs, hs, xf, xg, zb, yb, db, vb, u, part, recv, dh, dh_sent, dh_recv,
     zf, yf, u_f, part_f, recv_f, back, sent, sent_f, load_sem, ag_send, ag_recv, rs_send, rs_recv, y_send, y_recv,
     f_send, f_recv, b_send, b_recv,
 ):
@@ -168,9 +168,11 @@
         pltpu.make_async_copy(xs_hbm.at[0], xs, load_sem.at[4]),
         pltpu.make_async_copy(last_hbm.at[me], last, load_sem.at[5]),
         pltpu.make_async_copy(shuffle_hbm, shuffle, load_sem.at[6]),
+        pltpu.make_async_copy(x_hbm, x_ref, load_sem.at[7]),
     ]
-    for index in (6, 0, 1, 2, 3, 4, 5):
+    for index in (7, 6, 0, 1, 2, 3, 4, 5):
         loads[index].start()
+    loads[7].wait()
 
     def spread(j, carry):
         for n in range(4):
@@ -322,7 +324,13 @@
         write(sent, q, base + k + 1, values)
         reduce_copy(q, k + 1, long).start()
 
+    def gather_sent(q):
+        for k in range(7):
+            gather_copy(q, k % 4, k < 4).wait_send()
+
     def reduce_end(q):
+        for k in range(7):
+            reduce_copy(q, k % 4, k < 4).wait_send()
         values = add(share(part, me, q), add(read(recv, q, 3), read(recv, q, 6)))
         for (rows, lanes), value in zip(lines_of, values):
             xf[lanes.start // 128, q * TIMES + rows.start : q * TIMES + rows.start + 16, :] = value
@@ -379,6 +387,13 @@
             part_f[me, h, rows, lanes] = value
         for o in (1, 2, 3):
             back_copy(h, o).start()
+        for o in (1, 2, 3):
+            batch_copy(h, o).wait_send()
+        for slot in range(7):
+            if h:
+                pair_copy(h, slot).wait_send()
+            else:
+                chain_copy(h, slot % 4, slot < 4).wait_send()
         here = pl.multiple_of(batch * 8, 8)
         back[pl.ds(pl.multiple_of((HALF * h + batch) * 8, 8), 8), :] = part_f[
             me, h, pl.ds(here, 8), :
@@ -475,6 +490,7 @@
         elif kind == "UE":
             need(5)
             finish(vb.at[q // HALF], q % HALF, u.at[q % HALF], part, q)
+            gather_sent(q)
         elif kind in ("Rl", "Rr"):
             reduce_hop(q, k, kind == "Rl")
         elif kind == "X":
@@ -515,7 +531,7 @@
 
     for h in range(2):
         for o in (1, 2, 3):
-            back_copy(h, o).wait_recv()
+            back_copy(h, o).wait()
     high, low = split(back[...])
     rest = (back[...] - high.astype(F32) - low.astype(F32)).astype(BF16)
     lines = sum(
@@ -526,23 +542,6 @@
         for j in range(8):
             start = j * COLS + n * 128
             fl_ref[:, start : start + 128] = xf[n, pl.ds(j, CH, stride=8), :]
-
-    for q in range(CH):
-        for k in range(4):
-            gather_copy(q, k, True).wait_send()
-            reduce_copy(q, k, True).wait_send()
-            if k < 3:
-                gather_copy(q, k, False).wait_send()
-                reduce_copy(q, k, False).wait_send()
-    for h in range(2):
-        for slot in range(7):
-            if h:
-                pair_copy(h, slot).wait_send()
-            else:
-                chain_copy(h, slot % 4, slot < 4).wait_send()
-        for o in (1, 2, 3):
-            batch_copy(h, o).wait_send()
-            back_copy(h, o).wait_send()
 
 
 def hand_on(in_a, in_b, out_a, out_b):
@@ -562,9 +561,10 @@
     results = pl.pallas_call(
         kernel,
         out_shape=out_shape,
-        in_specs=[vmem] + [anywhere] * 7,
+        in_specs=[anywhere] * 8,
         out_specs=(vmem, vmem),
         scratch_shapes=[
+            pltpu.VMEM((1, CH, TIMES * COLS), BF16),
             pltpu.VMEM((8, 768, 256), BF16),
             pltpu.VMEM((256, 256), BF16),
             pltpu.VMEM((256, 384), BF16),
@@ -592,7 +592,7 @@
             pltpu.VMEM((CH * 8, COLS), F32),
             pltpu.VMEM((CH, 7, 9, 16, 128), BF16),
             pltpu.VMEM((2, 7, 9, 16, 128), BF16),
-            dma((7,)),
+            dma((8,)),
             dma((CH, 7)), dma((CH, 7)),
             dma((CH, 7)), dma((CH, 7)),
             dma((2, 3)), dma((2, 3)),

time: 70.8 us -> 69.6 us (0.983)
  Pallas kernels: 70 us -> 68.8 us
    pallas_call x1, Pallas kernels: 68.2 us -> 67.1 us  [on_device(): pl.pallas_call(kernel, out_shape=out_shape, in_specs=[anywhere] * 8, out_...]
where the time goes in v6:
time: 69.6 us; the launch traced here: 69.5 us
  Pallas kernels  68.8 us (99%)
    pallas_call x1, Pallas kernels, on_device(): pl.pallas_call(kernel, out_shape=out_shape, in_specs=[anywhere] * 8, out_...  67.1 us
    pallas_call x1, Pallas kernels, on_device(): pl.pallas_call(hand_on, out_shape=out_shape, in_specs=[vmem] * 2, out_spe...  1.74 us

profile of v6, /device:TPU:2, one launch (start us, length us, event | category | flops | bytes accessed | tf_op | source)
XLA Modules:
  0.0 69.5 jit_solution(9917960961534125068)
XLA Ops:
  0.6 67.1 %shard_map.95 = (bf16[1,8,16384]{2,1,0:T(8,128)(2,1)}, f32[8,4096]{1,0:T(8,128)}) custom-call(bf16[1,8,16384]{2,1,0:T(8,128)(2,1)} %x_hbm.1, f32[1,2,8,64,512]{4,3,2,1,0:T(8,128)} %xs_hbm.1, f32[2,8,64,512]{3,2,1,0:T(8,128)} %hs_hbm.1, bf16[8,768,256]{2,1,0:T(8,128)(2,1)} %constant.10.clone.wide_hbm, bf16[8,256,256]{2,1,0:T(8,128)(2,1)} %constant.11.clone.first_hbm, ...), custom_call_target="tpu_custom_call" | custom-call | tf_op jit(solution)/shard_map/pallas_call | solution.py:561
  67.7 1.7 %shard_map.96 = (bf16[1,8,16384]{2,1,0:T(8,128)(2,1)}, f32[8,4096]{1,0:T(8,128)}) custom-call(bf16[1,8,16384]{2,1,0:T(8,128)(2,1)} %get-tuple-element.4.in_a, f32[8,4096]{1,0:T(8,128)} %get-tuple-element.5.in_b), custom_call_target="tpu_custom_call" | custom-call | tf_op jit(solution)/shard_map/pallas_call | solution.py:606

commit v7 on v6

--- a/solution.py
+++ b/solution.py
@@ -24,36 +24,35 @@
 LANES = 128
 NEAR = (1, -1, 2, -2, 3, -3)
 CHAIN_WAY = -1
-LONG_WAY = (1, 1, 1, 1, -1, -1, -1, -1)
+LONG_WAY = (1, 1, 1, -1, 1, -1, -1, -1)
 ORDER = (
     ("gs", 0), ("gs", 1), ("gs", 2), ("gs", 3), ("gl", 0, 0), ("gr", 0, 0), ("gl", 1, 0),
-    ("gr", 1, 0), ("gl", 2, 0), ("gr", 2, 0), ("gl", 3, 0), ("gr", 3, 0), ("gl", 0, 1),
-    ("gr", 0, 1), ("gl", 1, 1), ("gr", 1, 1), ("gl", 2, 1), ("gr", 2, 1), ("gl", 3, 1), ("gs", 5),
-    ("gr", 3, 1), ("gl", 0, 2), ("gr", 0, 2), ("gl", 1, 2), ("gr", 1, 2), ("gs", 4), ("gs", 7),
-    ("gl", 2, 2), ("gr", 2, 2), ("gl", 3, 2), ("gs", 6), ("gl", 5, 0), ("gr", 5, 0), ("gr", 3, 2),
-    ("gl", 0, 3), ("A", 0), ("gl", 4, 0), ("gl", 1, 3), ("A", 1), ("gl", 7, 0), ("gr", 4, 0),
-    ("gl", 6, 0), ("gr", 7, 0), ("gl", 5, 1), ("gl", 2, 3), ("A", 2), ("gl", 4, 1), ("gl", 3, 3),
-    ("A", 3), ("B", 0), ("gl", 6, 1), ("gr", 6, 0), ("gl", 7, 1), ("gr", 5, 1), ("C", 0),
-    ("gl", 5, 2), ("gr", 4, 1), ("Y", 0), ("gl", 4, 2), ("D", 0), ("gr", 7, 1), ("UE", 0),
-    ("gl", 6, 2), ("gr", 6, 1), ("Rl", 0, -1), ("Rr", 0, -1), ("UE", 1), ("gl", 7, 2),
-    ("gr", 5, 2), ("Rl", 1, -1), ("Rr", 1, -1), ("UE", 2), ("gl", 5, 3), ("Rl", 2, -1),
-    ("Rr", 2, -1), ("gr", 4, 2), ("A", 5), ("gl", 4, 3), ("A", 4), ("gr", 7, 2), ("UE", 3),
-    ("gl", 6, 3), ("gr", 6, 2), ("Rl", 3, -1), ("Rr", 3, -1), ("A", 6), ("Rr", 0, 0), ("Rl", 0, 0),
-    ("gl", 7, 3), ("A", 7), ("Rl", 1, 0), ("B", 1), ("Rr", 1, 0), ("Rl", 2, 0), ("C", 1),
-    ("Rl", 3, 0), ("Rr", 2, 0), ("Rr", 3, 0), ("Y", 1), ("Rl", 0, 1), ("F", 0), ("Rr", 0, 1),
-    ("Rl", 1, 1), ("Rr", 1, 1), ("Rl", 2, 1), ("Fs", 0), ("D", 1), ("Rl", 3, 1), ("Rr", 2, 1),
-    ("Rl", 0, 2), ("Rr", 3, 1), ("UE", 4), ("Rl", 4, -1), ("Rr", 4, -1), ("UE", 5), ("Rl", 1, 2),
-    ("Rl", 5, -1), ("Rr", 5, -1), ("Rr", 0, 2), ("UE", 6), ("Rl", 2, 2), ("Rl", 6, -1),
-    ("Rr", 6, -1), ("UE", 7), ("Fl", 0, 0), ("Fr", 0, 0), ("Rl", 7, -1), ("Rr", 7, -1),
-    ("Rr", 1, 2), ("Rl", 3, 2), ("Rr", 2, 2), ("Rr", 3, 2), ("Rl", 0, 3), ("X", 0), ("Rl", 4, 0),
-    ("F", 1), ("Fs", 1), ("Rl", 6, 0), ("Rr", 4, 0), ("Rl", 5, 0), ("Rr", 5, 0), ("Rl", 1, 3),
-    ("Fl", 0, 1), ("Rl", 2, 3), ("X", 1), ("X", 2), ("Rl", 7, 0), ("Rr", 6, 0), ("Rl", 4, 1),
-    ("Fr", 0, 1), ("Fc", 1), ("Rr", 7, 0), ("Rl", 3, 3), ("X", 3), ("Rl", 6, 1), ("Fa", 1),
-    ("Rl", 5, 1), ("Fb", 1), ("Fl", 0, 2), ("Rr", 4, 1), ("Rl", 7, 1), ("Rr", 5, 1), ("Rl", 4, 2),
-    ("Rr", 6, 1), ("Fr", 0, 2), ("Rr", 7, 1), ("Rl", 6, 2), ("Rl", 5, 2), ("Fl", 0, 3),
-    ("Fend", 0), ("Rl", 7, 2), ("Fend", 1), ("Rl", 4, 3), ("Rr", 4, 2), ("X", 4), ("Rl", 6, 3),
-    ("Rr", 5, 2), ("Rl", 5, 3), ("Rr", 6, 2), ("X", 5), ("X", 6), ("Rl", 7, 3), ("Rr", 7, 2),
-    ("X", 7),
+    ("gr", 1, 0), ("gl", 2, 0), ("gr", 2, 0), ("gl", 3, 0), ("gs", 4), ("gr", 3, 0), ("gl", 0, 1),
+    ("gr", 0, 1), ("gl", 1, 1), ("gr", 1, 1), ("gl", 2, 1), ("gr", 2, 1), ("gl", 4, 0),
+    ("gl", 3, 1), ("gs", 7), ("gr", 4, 0), ("gr", 3, 1), ("gr", 0, 2), ("gl", 0, 2), ("gr", 1, 2),
+    ("gl", 1, 2), ("gs", 6), ("gr", 2, 2), ("gl", 2, 2), ("gs", 5), ("gl", 4, 1), ("gl", 3, 2),
+    ("gl", 7, 0), ("gr", 7, 0), ("gr", 4, 1), ("gr", 3, 2), ("gl", 6, 0), ("gl", 0, 3), ("A", 0),
+    ("gl", 1, 3), ("gl", 5, 0), ("A", 1), ("gr", 6, 0), ("gl", 3, 3), ("A", 3), ("gl", 7, 1),
+    ("gl", 2, 3), ("A", 2), ("B", 0), ("gr", 4, 2), ("gr", 5, 0), ("gl", 6, 1), ("gl", 4, 2),
+    ("C", 0), ("gr", 7, 1), ("gl", 5, 1), ("Y", 0), ("D", 0), ("gr", 6, 1), ("gl", 7, 2),
+    ("UE", 0), ("Rl", 0, -1), ("gr", 5, 1), ("gl", 6, 2), ("Rr", 0, -1), ("UE", 1), ("gl", 4, 3),
+    ("Rl", 1, -1), ("gl", 5, 2), ("Rr", 1, -1), ("A", 4), ("UE", 2), ("gr", 7, 2), ("Rl", 2, -1),
+    ("Rr", 2, -1), ("UE", 3), ("gr", 6, 2), ("gl", 7, 3), ("Rl", 3, -1), ("Rr", 3, -1), ("A", 7),
+    ("Rl", 0, 0), ("gl", 6, 3), ("A", 6), ("gr", 5, 2), ("Rr", 0, 0), ("Rl", 1, 0), ("gl", 5, 3),
+    ("A", 5), ("B", 1), ("Rr", 1, 0), ("Rl", 2, 0), ("C", 1), ("Rr", 3, 0), ("Rr", 2, 0),
+    ("Rl", 0, 1), ("Rl", 3, 0), ("F", 0), ("Rr", 0, 1), ("Fs", 0), ("Rl", 1, 1), ("Rr", 1, 1),
+    ("Rl", 2, 1), ("Y", 1), ("D", 1), ("Rr", 3, 1), ("Rr", 2, 1), ("Rl", 0, 2), ("Rl", 3, 1),
+    ("UE", 4), ("Rl", 4, -1), ("Rr", 4, -1), ("UE", 5), ("Fr", 0, 0), ("Rl", 5, -1), ("Rr", 5, -1),
+    ("Fl", 0, 0), ("Rl", 1, 2), ("UE", 6), ("Rl", 6, -1), ("Rr", 6, -1), ("Rl", 2, 2), ("UE", 7),
+    ("Rl", 7, -1), ("Rr", 7, -1), ("Rr", 0, 2), ("Rr", 3, 2), ("Rr", 1, 2), ("Rr", 2, 2),
+    ("Rl", 3, 2), ("Rl", 0, 3), ("X", 0), ("Rr", 4, 0), ("Rl", 4, 0), ("Rl", 5, 0), ("Fr", 0, 1),
+    ("Fl", 0, 1), ("Rr", 5, 0), ("Rl", 6, 0), ("F", 1), ("Fs", 1), ("Rr", 6, 0), ("Rl", 7, 0),
+    ("Rl", 3, 3), ("Rl", 1, 3), ("Rr", 4, 1), ("Rl", 2, 3), ("Rr", 7, 0), ("X", 1), ("X", 2),
+    ("X", 3), ("Rl", 5, 1), ("Rl", 4, 1), ("Fl", 0, 2), ("Fr", 0, 2), ("Rl", 6, 1), ("Rr", 5, 1),
+    ("Fc", 1), ("Fa", 1), ("Fb", 1), ("Rl", 7, 1), ("Rr", 6, 1), ("Rr", 4, 2), ("Rr", 7, 1),
+    ("Rl", 5, 2), ("Rl", 4, 2), ("Fl", 0, 3), ("Fend", 0), ("Rr", 5, 2), ("Rl", 6, 2),
+    ("Rl", 7, 2), ("Fend", 1), ("Rl", 5, 3), ("X", 5), ("Rr", 6, 2), ("Rl", 6, 3), ("X", 6),
+    ("Rr", 7, 2), ("Rl", 4, 3), ("X", 4), ("Rl", 7, 3), ("X", 7),
 )
 
 
@@ -167,11 +166,12 @@
         pltpu.make_async_copy(hs_hbm, hs, load_sem.at[3]),
         pltpu.make_async_copy(xs_hbm.at[0], xs, load_sem.at[4]),
         pltpu.make_async_copy(last_hbm.at[me], last, load_sem.at[5]),
-        pltpu.make_async_copy(shuffle_hbm, shuffle, load_sem.at[6]),
+        pltpu.make_async_copy(shuffle_hbm.at[0], shuffle.at[0], load_sem.at[6]),
         pltpu.make_async_copy(x_hbm, x_ref, load_sem.at[7]),
+        pltpu.make_async_copy(shuffle_hbm.at[1], shuffle.at[1], load_sem.at[8]),
     ]
-    for index in (7, 6, 0, 1, 2, 3, 4, 5):
-        loads[index].start()
+    loads[7].start()
+    loads[6].start()
     loads[7].wait()
 
     def spread(j, carry):
@@ -180,7 +180,7 @@
             xf[n, pl.ds(j, CH, stride=TIMES), :] = x_ref[0, :, lanes].astype(F32)
         return carry
 
-    lax.fori_loop(0, TIMES, spread, 0)
+    lax.fori_loop(0, TIMES, spread, 0, unroll=8)
     mine = pl.multiple_of(me * TIMES, TIMES)
     loads[6].wait()
     rows = jnp.concatenate([xf[n].astype(BF16) for n in range(4)], axis=1)
@@ -513,8 +513,14 @@
         elif kind == "Fend":
             pair_end(q)
 
+    started = False
     for task in ORDER:
+        if task[0] != "gs" and not started:
+            for index in (0, 1, 2, 3, 4, 5, 8):
+                loads[index].start()
+            started = True
         run(*task)
+    need(8)
 
     rows = jnp.concatenate([xf[n].astype(BF16) for n in range(4)], axis=1)
     rows = jnp.dot(rows, shuffle[1], preferred_element_type=F32)
@@ -527,7 +533,7 @@
             in_ref[0, :, lanes] = xf[n, pl.ds(j, CH, stride=TIMES), :].astype(BF16)
         return carry
 
-    lax.fori_loop(0, TIMES, collect, 0)
+    lax.fori_loop(0, TIMES, collect, 0, unroll=8)
 
     for h in range(2):
         for o in (1, 2, 3):
@@ -544,9 +550,17 @@
             fl_ref[:, start : start + 128] = xf[n, pl.ds(j, CH, stride=8), :]
 
 
-def hand_on(in_a, in_b, out_a, out_b):
-    out_a[...] = in_a[...]
-    out_b[...] = in_b[...]
+def hand_on(in_a, in_b, out_a, out_b, held_a, held_b, sems):
+    arrays = ((in_a, held_a, out_a), (in_b, held_b, out_b))
+    inward = [pltpu.make_async_copy(a, b, sems.at[i]) for i, (a, b, _) in enumerate(arrays)]
+    outward = [pltpu.make_async_copy(b, c, sems.at[2 + i]) for i, (_, b, c) in enumerate(arrays)]
+    for copy in inward:
+        copy.start()
+    for copy, after in zip(inward, outward):
+        copy.wait()
+        after.start()
+    for copy in outward:
+        copy.wait()
 
 
 def on_device(grad_out, input_spectrum, filter_spectrum):
@@ -592,7 +606,7 @@
             pltpu.VMEM((CH * 8, COLS), F32),
             pltpu.VMEM((CH, 7, 9, 16, 128), BF16),
             pltpu.VMEM((2, 7, 9, 16, 128), BF16),
-            dma((8,)),
+            dma((9,)),
             dma((CH, 7)), dma((CH, 7)),
             dma((CH, 7)), dma((CH, 7)),
             dma((2, 3)), dma((2, 3)),
@@ -606,8 +620,14 @@
     return pl.pallas_call(
         hand_on,
         out_shape=out_shape,
-        in_specs=[vmem] * 2,
-        out_specs=(vmem,) * 2,
+        in_specs=[anywhere] * 2,
+        out_specs=(anywhere,) * 2,
+        scratch_shapes=[
+            pltpu.VMEM((1, CH, TIMES * COLS), BF16),
+            pltpu.VMEM((CH, TIMES * COLS // BATCHES), F32),
+            dma((4,)),
+        ],
+        compiler_params=pltpu.CompilerParams(vmem_limit_bytes=56 * 1024 * 1024),
     )(*results)
 
 

time: 69.6 us -> 69.3 us (level)
  no operation moved by 1% of the time
where the time goes in v7:
time: 69.3 us; the launch traced here: 69.1 us
  Pallas kernels  68.3 us (99%)
  between operations  0.8 us (1%)
    pallas_call x1, Pallas kernels, on_device(): pl.pallas_call(kernel, out_shape=out_shape, in_specs=[anywhere] * 8, out_...  66.6 us
    pallas_call x1, Pallas kernels, on_device(): pl.pallas_call(hand_on, out_shape=out_shape, in_specs=[anywhere] * 2, out...  1.73 us

profile of v7, /device:TPU:2, one launch (start us, length us, event | category | flops | bytes accessed | tf_op | source)
XLA Modules:
  0.0 69.1 jit_solution(5938732592532816031)
XLA Ops:
  0.6 66.6 %shard_map.95 = (bf16[1,8,16384]{2,1,0:T(8,128)(2,1)}, f32[8,4096]{1,0:T(8,128)}) custom-call(bf16[1,8,16384]{2,1,0:T(8,128)(2,1)} %x_hbm.1, f32[1,2,8,64,512]{4,3,2,1,0:T(8,128)} %xs_hbm.1, f32[2,8,64,512]{3,2,1,0:T(8,128)} %hs_hbm.1, bf16[8,768,256]{2,1,0:T(8,128)(2,1)} %constant.10.clone.wide_hbm, bf16[8,256,256]{2,1,0:T(8,128)(2,1)} %constant.11.clone.first_hbm, ...), custom_call_target="tpu_custom_call" | custom-call | tf_op jit(solution)/shard_map/pallas_call | solution.py:575
  67.2 1.7 %shard_map.96 = (bf16[1,8,16384]{2,1,0:T(8,128)(2,1)}, f32[8,4096]{1,0:T(8,128)}) custom-call(bf16[1,8,16384]{2,1,0:T(8,128)(2,1)} %get-tuple-element.4.in_a, f32[8,4096]{1,0:T(8,128)} %get-tuple-element.5.in_b), custom_call_target="tpu_custom_call" | custom-call | tf_op jit(solution)/shard_map/pallas_call | solution.py:620

commit v8 on v7

--- a/solution.py
+++ b/solution.py
@@ -183,7 +183,7 @@
     lax.fori_loop(0, TIMES, spread, 0, unroll=8)
     mine = pl.multiple_of(me * TIMES, TIMES)
     loads[6].wait()
-    rows = jnp.concatenate([xf[n].astype(BF16) for n in range(4)], axis=1)
+    rows = jnp.concatenate([xf[n, 0 : CH * TIMES, :].astype(BF16) for n in range(4)], axis=1)
     rows = jnp.dot(rows, shuffle[0], preferred_element_type=F32).astype(BF16)
     for c in range(CH):
         xg[c, pl.ds(mine, TIMES), :] = rows[c * TIMES : (c + 1) * TIMES, :]
@@ -522,10 +522,10 @@
         run(*task)
     need(8)
 
-    rows = jnp.concatenate([xf[n].astype(BF16) for n in range(4)], axis=1)
+    rows = jnp.concatenate([xf[n, 0 : CH * TIMES, :].astype(BF16) for n in range(4)], axis=1)
     rows = jnp.dot(rows, shuffle[1], preferred_element_type=F32)
     for n in range(4):
-        xf[n] = rows[:, n * 128 : (n + 1) * 128]
+        xf[n, 0 : CH * TIMES, :] = rows[:, n * 128 : (n + 1) * 128]
 
     def collect(j, carry):
         for n in range(4):
@@ -586,7 +586,7 @@
             pltpu.VMEM((2, COLS, COLS), BF16),
             pltpu.VMEM((2, CH, ROWS, COLS), F32),
             pltpu.VMEM((2, CH, ROWS, COLS), F32),
-            pltpu.VMEM((4, CH * TIMES, 128), F32),
+            pltpu.VMEM((4, (CH + 1) * TIMES, 128), F32),
             pltpu.VMEM((CH, SHARDS * TIMES, COLS), BF16),
             pltpu.VMEM((2, 4, HALF * ROWS, 768), BF16),
             pltpu.VMEM((2, 4, HALF * ROWS, 256), F32),

time: 69.3 us -> 69.3 us (level)
  no operation moved by 1% of the time
where the time goes in v8:
time: 69.3 us; the launch traced here: 69.1 us
  Pallas kernels  68.3 us (99%)
  between operations  0.8 us (1%)
    pallas_call x1, Pallas kernels, on_device(): pl.pallas_call(kernel, out_shape=out_shape, in_specs=[anywhere] * 8, out_...  66.6 us
    pallas_call x1, Pallas kernels, on_device(): pl.pallas_call(hand_on, out_shape=out_shape, in_specs=[anywhere] * 2, out...  1.73 us

profile of v8, /device:TPU:2, one launch (start us, length us, event | category | flops | bytes accessed | tf_op | source)
XLA Modules:
  0.0 69.1 jit_solution(14083455102505393599)
XLA Ops:
  0.6 66.6 %shard_map.95 = (bf16[1,8,16384]{2,1,0:T(8,128)(2,1)}, f32[8,4096]{1,0:T(8,128)}) custom-call(bf16[1,8,16384]{2,1,0:T(8,128)(2,1)} %x_hbm.1, f32[1,2,8,64,512]{4,3,2,1,0:T(8,128)} %xs_hbm.1, f32[2,8,64,512]{3,2,1,0:T(8,128)} %hs_hbm.1, bf16[8,768,256]{2,1,0:T(8,128)(2,1)} %constant.10.clone.wide_hbm, bf16[8,256,256]{2,1,0:T(8,128)(2,1)} %constant.11.clone.first_hbm, ...), custom_call_target="tpu_custom_call" | custom-call | tf_op jit(solution)/shard_map/pallas_call | solution.py:575
  67.2 1.7 %shard_map.96 = (bf16[1,8,16384]{2,1,0:T(8,128)(2,1)}, f32[8,4096]{1,0:T(8,128)}) custom-call(bf16[1,8,16384]{2,1,0:T(8,128)(2,1)} %get-tuple-element.4.in_a, f32[8,4096]{1,0:T(8,128)} %get-tuple-element.5.in_b), custom_call_target="tpu_custom_call" | custom-call | tf_op jit(solution)/shard_map/pallas_call | solution.py:620
